TPU v7x, 32 devices: a whole 2x2x4 slice. The times are simulated.
32 devices in a mesh: ctx: 8 (over z, y), head: 4 (over x, core).
Axes of the slice: x: 2, y: 2, z: 4, core: 2. Of those that a mesh axis runs over, the one named last changes fastest.
Arguments:
- queries: bfloat16 [8, 512, 3072], P('ctx', None, 'head'), may hold values from -5 to 5
- key_rows: bfloat16 [8, 512, 3072], P('ctx', None, 'head'), may hold values from -5 to 5
- value_rows: bfloat16 [8, 512, 3072], P('ctx', None, 'head'), may hold values from -6 to 6
- out_grad: bfloat16 [8, 512, 3072], P('ctx', None, 'head'), may hold values from -6 to 6
- head_kind: int32 [24], replicated, may hold values from 0 to 1, as said below
- frame_band: int32 [24], replicated, may hold values from 1 to 7, as said below
Outputs:
- attended: bfloat16 [8, 512, 3072], P('ctx', None, 'head')
- query_grad: bfloat16 [8, 512, 3072], P('ctx', None, 'head')
- key_grad: bfloat16 [8, 512, 3072], P('ctx', None, 'head')
- value_grad: bfloat16 [8, 512, 3072], P('ctx', None, 'head')
Inputs may be any that keep to these rules, and one draw needn't show every extreme that they name: `head_kind`: exactly 8 entries are 1. `frame_band`: entries of spatial heads are not used; some temporal head has the value 8 - 1.
All inputs are finite; a program needn't handle non-finite values.
Results may differ from a plain program's by a relative error of at most 0.024.
Values may be sent and summed in bfloat16 or wider, within the bound.
No kernel may reach another device: no remote copies, remote signals or barrier semaphores. Data moves between devices by JAX's collectives and lax.ppermute only.
A program may use at most 64 MiB of HBM per device.

v0:
```python
import functools

import jax
import jax.numpy as jnp
from jax import lax
from jax.experimental import pallas as pl
from jax.experimental.pallas import tpu as pltpu
from jax.sharding import PartitionSpec as P

DH = 128
SCALE = DH ** (-0.5)
SPATIAL, TEMPORAL = 1, 0
MASKED = -1e30
F32 = jnp.float32
BF16 = jnp.bfloat16
MIB = 1024 * 1024


def head_at(kind_ref, heads, kind, slot):
    found, seen = jnp.int32(0), jnp.int32(0)
    for head in range(heads):
        hit = kind_ref[head] == kind
        found = jnp.where(jnp.logical_and(hit, seen == slot), jnp.int32(head), found)
        seen = seen + hit.astype(jnp.int32)
    return found


def dot_nt(a, b):
    return lax.dot_general(a, b, (((1,), (1,)), ((), ())), preferred_element_type=F32)


def dot_nn(a, b):
    return lax.dot_general(a, b, (((1,), (0,)), ((), ())), preferred_element_type=F32)


def dot_tn(a, b):
    return lax.dot_general(a, b, (((0,), (0,)), ((), ())), preferred_element_type=F32)


def params(mib=32):
    return pltpu.CompilerParams(
        dimension_semantics=("arbitrary",), vmem_limit_bytes=mib * MIB
    )


def cost(flops, moved):
    return pl.CostEstimate(flops=int(flops), bytes_accessed=int(moved), transcendentals=0)


def column_spec(count, heads, kind):
    return pl.BlockSpec((count, DH), lambda i, kind_ref: (0, head_at(kind_ref, heads, kind, i)))


def head_columns(kind_ref, heads, kind, slot):
    return pl.ds(pl.multiple_of(head_at(kind_ref, heads, kind, slot) * DH, DH), DH)


def copy_all(pairs, sems):
    copies = [pltpu.make_async_copy(*pair, sems.at[i]) for i, pair in enumerate(pairs)]
    for copy in copies:
        copy.start()
    for copy in copies:
        copy.wait()


def pack(kinds, arrays, slots, heads):
    frames, rows, _ = arrays[0].shape
    others = heads - slots
    shapes = []
    if slots > 0:
        shapes.append(jax.ShapeDtypeStruct((frames, 4, slots, rows, DH), BF16))
    if others > 0:
        shapes.append(jax.ShapeDtypeStruct((others, 2, frames, rows, DH), BF16))

    def kernel(kind_ref, *refs):
        ins, outs, sems = refs[:4], refs[4:-1], refs[-1]
        pairs = []
        for slot in range(others):
            cols = head_columns(kind_ref, heads, SPATIAL, slot)
            for place, ref in enumerate(ins[1:3]):
                pairs.append((ref.at[:, :, cols], outs[-1].at[slot, place]))
        for slot in range(slots):
            cols = head_columns(kind_ref, heads, TEMPORAL, slot)
            for place, ref in enumerate(ins):
                pairs.append((ref.at[:, :, cols], outs[0].at[:, place, slot]))
        copy_all(pairs, sems)

    outs = pl.pallas_call(
        kernel,
        out_shape=shapes,
        in_specs=[pl.BlockSpec(memory_space=pltpu.SMEM)] + [pl.BlockSpec(memory_space=pl.ANY)] * 4,
        out_specs=[pl.BlockSpec(memory_space=pl.ANY)] * len(shapes),
        scratch_shapes=[pltpu.SemaphoreType.DMA((4 * slots + 2 * others,))],
        compiler_params=pltpu.CompilerParams(vmem_limit_bytes=MIB),
        cost_estimate=cost(0, 4 * (4 * slots + 2 * others) * frames * rows * DH),
        name="pack",
    )(kinds, *arrays)
    return (outs[0] if slots > 0 else None), (outs[-1] if others > 0 else None)


def temporal(kinds, bands, rows_in, heads):
    frames, _, slots, rows, _ = rows_in.shape
    group = 16
    size = frames * group

    def kernel(kind_ref, band_ref, in_ref, out_ref):
        band = band_ref[head_at(kind_ref, heads, TEMPORAL, pl.program_id(0))]
        row = lax.broadcasted_iota(jnp.int32, (size, size), 0)
        col = lax.broadcasted_iota(jnp.int32, (size, size), 1)
        same = lax.rem(row, group) == lax.rem(col, group)
        near = jnp.abs(lax.div(row, group) - lax.div(col, group)) <= band
        allowed = jnp.logical_and(same, near)
        parts = [slice(start, start + group) for start in range(0, rows, group)]
        qs, ks, vs, gs = (
            [in_ref[:, place, 0, part].reshape(size, DH) for part in parts] for place in range(4)
        )
        scores = [jnp.where(allowed, dot_nt(q, k) * SCALE, MASKED) for q, k in zip(qs, ks)]
        dprobs = [dot_nt(g, v) for g, v in zip(gs, vs)]
        raised = [jnp.exp(x - jnp.max(x, axis=1, keepdims=True)) for x in scores]
        weights = [x * (1.0 / jnp.sum(x, axis=1, keepdims=True)) for x in raised]
        probs = [x.astype(BF16) for x in weights]
        attended = [dot_nn(x, v).astype(BF16) for x, v in zip(probs, vs)]
        deltas = [
            jnp.sum(g.astype(F32) * x.astype(F32), axis=1, keepdims=True)
            for g, x in zip(gs, attended)
        ]
        dscores = [
            (w * (dp - delta) * SCALE).astype(BF16)
            for w, dp, delta in zip(weights, dprobs, deltas)
        ]
        results = (
            attended,
            [dot_nn(x, k).astype(BF16) for x, k in zip(dscores, ks)],
            [dot_tn(x, q).astype(BF16) for x, q in zip(dscores, qs)],
            [dot_tn(x, g).astype(BF16) for x, g in zip(probs, gs)],
        )
        for place, result in enumerate(results):
            for part, value in zip(parts, result):
                out_ref[:, place, 0, part] = value.reshape(frames, group, DH)

    spec = pl.BlockSpec(
        (frames, 4, 1, rows, DH), lambda i, kind_ref, band_ref: (0, 0, i, 0, 0)
    )
    return pl.pallas_call(
        kernel,
        out_shape=jax.ShapeDtypeStruct(rows_in.shape, BF16),
        grid_spec=pltpu.PrefetchScalarGridSpec(
            num_scalar_prefetch=2, grid=(slots,), in_specs=[spec], out_specs=spec
        ),
        compiler_params=params(),
        cost_estimate=cost(12 * slots * rows * frames * size * DH, 4 * rows_in.size),
        name="temporal",
    )(kinds, bands, rows_in)


def unpack(kinds, rows_in, filled, heads):
    frames, _, slots, rows, _ = rows_in.shape

    def kernel(kind_ref, in_ref, *refs):
        outs, sems = refs[-5:-1], refs[-1]
        pairs = []
        for slot in range(slots):
            cols = head_columns(kind_ref, heads, TEMPORAL, slot)
            for place, ref in enumerate(outs):
                pairs.append((in_ref.at[:, place, slot], ref.at[:, :, cols]))
        copy_all(pairs, sems)

    return pl.pallas_call(
        kernel,
        out_shape=[jax.ShapeDtypeStruct((frames, rows, heads * DH), BF16)] * 4,
        in_specs=[pl.BlockSpec(memory_space=pltpu.SMEM)]
        + [pl.BlockSpec(memory_space=pl.ANY)] * (1 + len(filled)),
        out_specs=[pl.BlockSpec(memory_space=pl.ANY)] * 4,
        scratch_shapes=[pltpu.SemaphoreType.DMA((4 * slots,))],
        input_output_aliases={2 + place: place for place in range(len(filled))},
        compiler_params=pltpu.CompilerParams(vmem_limit_bytes=MIB),
        cost_estimate=cost(0, 4 * rows_in.size),
        name="unpack",
    )(kinds, rows_in, *filled)


def spatial(kinds, frame, arrays, prior, heads):
    count = arrays[0].shape[0]
    slots = prior.shape[0]
    chunk = 256

    def kernel(
        kind_ref, frame_ref, q_ref, k_ref, v_ref, g_ref, prior_ref,
        out_ref, qgrad_ref, own_ref, send_ref,
    ):
        has_prior = frame_ref[0] > 0
        k, v = k_ref[...], v_ref[...]
        k_prior, v_prior = prior_ref[0, 0], prior_ref[0, 1]
        k_own = v_own = k_send = v_send = None
        for start in range(0, count, chunk):
            part = slice(start, start + chunk)
            q, g = q_ref[part], g_ref[part]
            own = dot_nt(q, k) * SCALE
            before = jnp.where(has_prior, dot_nt(q, k_prior) * SCALE, MASKED)
            top = jnp.maximum(
                jnp.max(own, axis=1, keepdims=True), jnp.max(before, axis=1, keepdims=True)
            )
            own, before = jnp.exp(own - top), jnp.exp(before - top)
            total = jnp.sum(own, axis=1, keepdims=True) + jnp.sum(before, axis=1, keepdims=True)
            inverse = 1.0 / total
            own, before = own * inverse, before * inverse
            own_prob, before_prob = own.astype(BF16), before.astype(BF16)
            attended = (dot_nn(own_prob, v) + dot_nn(before_prob, v_prior)).astype(BF16)
            delta = jnp.sum(g.astype(F32) * attended.astype(F32), axis=1, keepdims=True)
            own_ds = (own * (dot_nt(g, v) - delta) * SCALE).astype(BF16)
            before_ds = (before * (dot_nt(g, v_prior) - delta) * SCALE).astype(BF16)
            out_ref[part] = attended
            qgrad_ref[part] = (dot_nn(own_ds, k) + dot_nn(before_ds, k_prior)).astype(BF16)
            terms = (
                dot_tn(own_ds, q), dot_tn(own_prob, g), dot_tn(before_ds, q), dot_tn(before_prob, g)
            )
            if start == 0:
                k_own, v_own, k_send, v_send = terms
            else:
                k_own, v_own = k_own + terms[0], v_own + terms[1]
                k_send, v_send = k_send + terms[2], v_send + terms[3]
        own_ref[0, 0], own_ref[0, 1] = k_own, v_own
        send_ref[0, 0], send_ref[0, 1] = k_send.astype(BF16), v_send.astype(BF16)

    columns = pl.BlockSpec(
        (count, DH), lambda i, kind_ref, frame_ref: (0, head_at(kind_ref, heads, SPATIAL, i))
    )
    pair = pl.BlockSpec((1, 2, count, DH), lambda i, kind_ref, frame_ref: (i, 0, 0, 0))
    whole = jax.ShapeDtypeStruct((count, heads * DH), BF16)
    return pl.pallas_call(
        kernel,
        out_shape=[
            whole,
            whole,
            jax.ShapeDtypeStruct(prior.shape, F32),
            jax.ShapeDtypeStruct(prior.shape, BF16),
        ],
        grid_spec=pltpu.PrefetchScalarGridSpec(
            num_scalar_prefetch=2,
            grid=(slots,),
            in_specs=[columns] * 4 + [pair],
            out_specs=[columns, columns, pair, pair],
        ),
        compiler_params=params(48),
        cost_estimate=cost(24 * slots * count * count * DH, 12 * 2 * slots * count * DH),
        name="spatial",
    )(kinds, frame, *arrays, prior)


def add_spatial(kinds, own, back, heads):
    slots, _, count, _ = own.shape

    def kernel(kind_ref, own_ref, back_ref, k_ref, v_ref):
        k_ref[...] = (own_ref[0, 0] + back_ref[0, 0].astype(F32)).astype(BF16)
        v_ref[...] = (own_ref[0, 1] + back_ref[0, 1].astype(F32)).astype(BF16)

    pair = pl.BlockSpec((1, 2, count, DH), lambda i, kind_ref: (i, 0, 0, 0))
    return pl.pallas_call(
        kernel,
        out_shape=[jax.ShapeDtypeStruct((count, heads * DH), BF16)] * 2,
        grid_spec=pltpu.PrefetchScalarGridSpec(
            num_scalar_prefetch=1,
            grid=(slots,),
            in_specs=[pair, pair],
            out_specs=[column_spec(count, heads, SPATIAL)] * 2,
        ),
        compiler_params=params(),
        cost_estimate=cost(0, 8 * own.size),
        name="add_spatial",
    )(kinds, own, back)


def passed_along(array, axis, by):
    length = lax.axis_size(axis)
    pairs = [(i, i + by) for i in range(length) if 0 <= i + by < length]
    return lax.ppermute(array, axis, pairs)


def branch(slots, heads, kinds, bands, frame, q, k, v, g):
    frames, rows, width = q.shape
    count = frames * rows
    exchange = functools.partial(
        lax.all_to_all, axis_name="ctx", split_axis=0, concat_axis=0, tiled=True
    )
    packed, pairs = pack(kinds, (q, k, v, g), slots, heads)
    filled = ()
    if slots > 0:
        framed = exchange(packed)
    if slots < heads:
        prior = passed_along(pairs, "ctx", 1).reshape(heads - slots, 2, count, DH)
        flat = [x.reshape(count, width) for x in (q, k, v, g)]
        attended, qgrad, own, send = spatial(kinds, frame, flat, prior, heads)
        if slots > 0:
            framed, send = lax.optimization_barrier((framed, send))
        back = passed_along(send, "ctx", -1)
        filled = (attended, qgrad, *add_spatial(kinds, own, back, heads))
        filled = tuple(x.reshape(q.shape) for x in filled)
    if slots > 0:
        returned = exchange(temporal(kinds, bands, framed, heads))
        filled = unpack(kinds, returned, filled, heads)
    return tuple(filled)


def body(queries, key_rows, value_rows, out_grad, head_kind, frame_band):
    frames = lax.axis_size("ctx")
    heads = queries.shape[2] // DH
    first = lax.axis_index("head") * heads
    kinds = lax.dynamic_slice_in_dim(head_kind, first, heads)
    bands = lax.dynamic_slice_in_dim(frame_band, first, heads)
    frame = lax.axis_index("ctx").astype(jnp.int32).reshape(1)
    count = queries.shape[1]
    arrays = [
        x.reshape(frames, count // frames, heads * DH)
        for x in (queries, key_rows, value_rows, out_grad)
    ]
    slots = jnp.sum((kinds == TEMPORAL).astype(jnp.int32))
    outs = lax.switch(
        slots,
        [functools.partial(branch, n, heads) for n in range(heads + 1)],
        kinds, bands, frame, *arrays,
    )
    return tuple(out.reshape(queries.shape) for out in outs)


def solution(mesh):
    rows = P("ctx", None, "head")
    return jax.shard_map(
        body,
        mesh=mesh,
        in_specs=(rows, rows, rows, rows, P(), P()),
        out_specs=(rows, rows, rows, rows),
        check_vma=False,
    )
```

profile of v0, /device:TPU:14, one launch (start us, length us, event | category | flops | bytes accessed | tf_op | source)
XLA Modules:
  0.0 152.0 jit_solution(3895565583294204198)
XLA Ops:
  0.6 0.7 dynamic_slice.7
  1.4 1.4 fusion
  3.4 148.4 %conditional.1 = (bf16[1,512,768]{2,1,0:T(8,128)(2,1)}, bf16[1,512,768]{2,1,0:T(8,128)(2,1)}, bf16[1,512,768]{2,1,0:T(8,128)(2,1)}, bf16[1,512,768]{2,1,0:T(8,128)(2,1)}) conditional(s32[]{:T(128)} %clamp.3, (bf16[1,512,768]{2,1,0:T(8,128)(2,1)}, bf16[1,512,768]{2,1,0:T(8,128)(2,1)}, bf16[1,512,768]{2,1,0:T(8,128)(2,1)}, ...), branch_computations={%region_1.0_spmd, %region_2.0_spmd, %region_3.0_spmd, %region_4.0_... | conditional | flops 4831838208 | bytes 57671912 | solution.py:317
  3.6 2.6 %pack.11 = (bf16[8,4,4,64,128]{4,3,2,1,0:T(8,128)(2,1)S(1)}, bf16[2,2,8,64,128]{4,3,2,1,0:T(8,128)(2,1)S(1)}) custom-call(s32[6]{0:T(128)S(1)} %get-tuple-element.261.kind_ref, bf16[8,64,768]{2,1,0:T(8,128)(2,1)} %bitcast.103, bf16[8,64,768]{2,1,0:T(8,128)(2,1)} %bitcast.121, bf16[8,64,768]{2,1,0:T(8,128)(2,1)} %bitcast.139, bf16[8,64,768]{2,1,0:T(8,128)(2,1)} %bitcast.157), custom_call_target="tpu_custom_call" | custom-call | bytes 5242880 | tf_op jit(solution)/shard_map/cond/branch_4_fun/pack/pallas_call | solution.py:88
  6.2 0.0 copy-start.5
  6.2 1.3 copy-done.5
  7.5 6.2 %all-to-all-start.6 = ((bf16[8,4,4,64,128]{4,3,2,1,0:T(8,128)(2,1)}), bf16[8,4,4,64,128]{4,3,2,1,0:T(8,128)(2,1)S(1)}, u32[]{:S(2)}, u32[]{:S(2)}) async-start(bf16[8,4,4,64,128]{4,3,2,1,0:T(8,128)(2,1)} %copy-done.5), calls=%async_computation.6 | async-start | bytes 4194304 | tf_op jit(solution)/shard_map/cond/branch_4_fun/all_to_all | solution.py:288
  13.8 3.4 %collective-permute-start.8 = (bf16[2,2,8,64,128]{4,3,2,1,0:T(8,128)(2,1)S(1)}, bf16[2,2,8,64,128]{4,3,2,1,0:T(8,128)(2,1)S(1)}, u32[]{:S(2)}, u32[]{:S(2)}) collective-permute-start(bf16[2,2,8,64,128]{4,3,2,1,0:T(8,128)(2,1)S(1)} %get-tuple-element.273), channel_id=1, source_target_pairs={{0,4},{4,8},{8,12},{12,16},{16,20},{20,24},{24,28},{1,5},{5,9},{9,... | collective-permute-start | bytes 1572872 | tf_op jit(solution)/shard_map/cond/branch_4_fun/ppermute | solution.py:276
  17.1 52.7 %collective-permute-done.8 = bf16[2,2,8,64,128]{4,3,2,1,0:T(8,128)(2,1)S(1)} collective-permute-done((bf16[2,2,8,64,128]{4,3,2,1,0:T(8,128)(2,1)S(1)}, bf16[2,2,8,64,128]{4,3,2,1,0:T(8,128)(2,1)S(1)}, u32[]{:S(2)}, u32[]{:S(2)}) %collective-permute-start.8) | collective-permute-done | bytes 524320 | tf_op jit(solution)/shard_map/cond/branch_4_fun/ppermute | solution.py:276
  69.8 7.7 %spatial.10 = (bf16[512,768]{1,0:T(8,128)(2,1)}, bf16[512,768]{1,0:T(8,128)(2,1)}, f32[2,2,512,128]{3,2,1,0:T(8,128)S(1)}, bf16[2,2,512,128]{3,2,1,0:T(8,128)(2,1)S(1)}) custom-call(s32[6]{0:T(128)S(1)} %get-tuple-element.261.kind_ref, s32[1]{0:T(128)} %get-tuple-element.268.frame_ref, bf16[512,768]{1,0:T(8,128)(2,1)} %bitcast.104, ...), custom_call_target="tpu_custom_call" | custom-call | flops 1610612736 | bytes 3145728 | tf_op jit(solution)/shard_map/cond/branch_4_fun/spatial/pallas_call | solution.py:230
  77.5 0.0 copy-start.11
  77.5 0.8 copy-done.11
  78.3 0.0 all-to-all-done.6.in_ref
  78.3 4.2 %temporal.9 = bf16[8,4,4,64,128]{4,3,2,1,0:T(8,128)(2,1)S(1)} custom-call(s32[6]{0:T(128)S(1)} %get-tuple-element.261.kind_ref, s32[6]{0:T(128)S(1)} %get-tuple-element.262.band_ref, bf16[8,4,4,64,128]{4,3,2,1,0:T(8,128)(2,1)S(1)} %all-to-all-done.6.in_ref), custom_call_target="tpu_custom_call" | custom-call | flops 402653184 | bytes 4194304 | tf_op jit(solution)/shard_map/cond/branch_4_fun/temporal/pallas_call | solution.py:144
  82.5 0.0 copy-start.1
  82.5 1.3 copy-done.1
  83.8 6.1 %all-to-all-start.7 = ((bf16[8,4,4,64,128]{4,3,2,1,0:T(8,128)(2,1)}), bf16[8,4,4,64,128]{4,3,2,1,0:T(8,128)(2,1)S(1)}, u32[]{:S(2)}, u32[]{:S(2)}) async-start(bf16[8,4,4,64,128]{4,3,2,1,0:T(8,128)(2,1)} %copy-done.1), calls=%async_computation.7 | async-start | bytes 4194304 | tf_op jit(solution)/shard_map/cond/branch_4_fun/all_to_all | solution.py:299
  89.9 2.5 %collective-permute-start.9 = (bf16[2,2,512,128]{3,2,1,0:T(8,128)(2,1)}, bf16[2,2,512,128]{3,2,1,0:T(8,128)(2,1)S(1)}, u32[]{:S(2)}, u32[]{:S(2)}) collective-permute-start(bf16[2,2,512,128]{3,2,1,0:T(8,128)(2,1)} %copy-done.11), channel_id=1, source_target_pairs={{4,0},{8,4},{12,8},{16,12},{20,16},{24,20},{28,24},{5,1},{9,5},{13... | collective-permute-start | bytes 1572872 | tf_op jit(solution)/shard_map/cond/branch_4_fun/ppermute | solution.py:276
  92.4 55.7 %collective-permute-done.9.back_ref = bf16[2,2,512,128]{3,2,1,0:T(8,128)(2,1)S(1)} collective-permute-done((bf16[2,2,512,128]{3,2,1,0:T(8,128)(2,1)}, bf16[2,2,512,128]{3,2,1,0:T(8,128)(2,1)S(1)}, u32[]{:S(2)}, u32[]{:S(2)}) %collective-permute-start.9) | collective-permute-done | bytes 524320 | tf_op jit(solution)/shard_map/cond/branch_4_fun/ppermute | solution.py:276
  148.1 1.4 add_spatial.10
  149.5 0.0 all-to-all-done.7.in_ref
  149.5 2.0 %unpack.9 = (bf16[8,64,768]{2,1,0:T(8,128)(2,1)}, bf16[8,64,768]{2,1,0:T(8,128)(2,1)}, bf16[8,64,768]{2,1,0:T(8,128)(2,1)}, bf16[8,64,768]{2,1,0:T(8,128)(2,1)}) custom-call(s32[6]{0:T(128)S(1)} %get-tuple-element.261.kind_ref, ...), custom_call_target="tpu_custom_call", output_to_operand_aliasing={{0}: (2, {}), {1}: (3, {}), {2}: (4, {}), {3}: (5, {})} | custom-call | bytes 4194304 | tf_op jit(solution)/shard_map/cond/branch_4_fun/unpack/pallas_call | solution.py:168
Async XLA Ops:
  6.2 1.3 copy-start.5
  7.5 70.8 %all-to-all-start.6 = ((bf16[8,4,4,64,128]{4,3,2,1,0:T(8,128)(2,1)}), bf16[8,4,4,64,128]{4,3,2,1,0:T(8,128)(2,1)S(1)}, u32[]{:S(2)}, u32[]{:S(2)}) async-start(bf16[8,4,4,64,128]{4,3,2,1,0:T(8,128)(2,1)} %copy-done.5), calls=%async_computation.6 | async-start | bytes 4194304 | tf_op jit(solution)/shard_map/cond/branch_4_fun/all_to_all | solution.py:288
  13.8 56.1 %collective-permute-start.8 = (bf16[2,2,8,64,128]{4,3,2,1,0:T(8,128)(2,1)S(1)}, bf16[2,2,8,64,128]{4,3,2,1,0:T(8,128)(2,1)S(1)}, u32[]{:S(2)}, u32[]{:S(2)}) collective-permute-start(bf16[2,2,8,64,128]{4,3,2,1,0:T(8,128)(2,1)S(1)} %get-tuple-element.273), channel_id=1, source_target_pairs={{0,4},{4,8},{8,12},{12,16},{16,20},{20,24},{24,28},{1,5},{5,9},{9,... | collective-permute-start | bytes 1572872 | tf_op jit(solution)/shard_map/cond/branch_4_fun/ppermute | solution.py:276
  77.5 0.8 copy-start.11
  82.5 1.3 copy-start.1
  83.8 65.7 %all-to-all-start.7 = ((bf16[8,4,4,64,128]{4,3,2,1,0:T(8,128)(2,1)}), bf16[8,4,4,64,128]{4,3,2,1,0:T(8,128)(2,1)S(1)}, u32[]{:S(2)}, u32[]{:S(2)}) async-start(bf16[8,4,4,64,128]{4,3,2,1,0:T(8,128)(2,1)} %copy-done.1), calls=%async_computation.7 | async-start | bytes 4194304 | tf_op jit(solution)/shard_map/cond/branch_4_fun/all_to_all | solution.py:299
  89.9 58.2 %collective-permute-start.9 = (bf16[2,2,512,128]{3,2,1,0:T(8,128)(2,1)}, bf16[2,2,512,128]{3,2,1,0:T(8,128)(2,1)S(1)}, u32[]{:S(2)}, u32[]{:S(2)}) collective-permute-start(bf16[2,2,512,128]{3,2,1,0:T(8,128)(2,1)} %copy-done.11), channel_id=1, source_target_pairs={{4,0},{8,4},{12,8},{16,12},{20,16},{24,20},{28,24},{5,1},{9,5},{13... | collective-permute-start | bytes 1572872 | tf_op jit(solution)/shard_map/cond/branch_4_fun/ppermute | solution.py:276
where the time goes:
time: 152 us
  waiting for transfers between devices  108 us (71%)
  starting transfers between devices  18.2 us (12%)
  Pallas kernels  17.8 us (12%)
  local copies, waits for them, and re-layouts  4.13 us (3%)
    ppermute x2, waiting for transfers between devices, passed_along(): return lax.ppermute(array, axis, pairs)  108 us
    pallas_call x1, Pallas kernels, spatial(): pl.pallas_call(kernel, out_shape=[whole, whole, jax.ShapeDtypeStruct(prio...  7.65 us
    all_to_all x1, starting transfers between devices, branch(): framed = exchange(packed)  6.22 us
    all_to_all x1, starting transfers between devices, branch(): returned = exchange(temporal(kinds, bands, framed, heads))  6.13 us
    ppermute x2, starting transfers between devices, passed_along(): return lax.ppermute(array, axis, pairs)  5.82 us
    pallas_call x1, Pallas kernels, temporal(): pl.pallas_call(kernel, out_shape=jax.ShapeDtypeStruct(rows_in.shape, BF16...  4.17 us
    cond x6, local copies, waits for them, and re-layouts  3.39 us
  transfers between devices with their start and end apart: 4, of which 2 were waited for; matrix products, arithmetic and copies ran while one was open for 0% of the time, Pallas kernels for 6%

commit v1 on v0

--- a/solution.py
+++ b/solution.py
@@ -55,47 +55,87 @@
     return pl.ds(pl.multiple_of(head_at(kind_ref, heads, kind, slot) * DH, DH), DH)
 
 
-def copy_all(pairs, sems):
-    copies = [pltpu.make_async_copy(*pair, sems.at[i]) for i, pair in enumerate(pairs)]
-    for copy in copies:
-        copy.start()
-    for copy in copies:
-        copy.wait()
-
-
-def pack(kinds, arrays, slots, heads):
+def staged_copies(triples, in_sems, out_sems):
+    loads = [pltpu.make_async_copy(x, y, in_sems.at[i]) for i, (x, y, _) in enumerate(triples)]
+    stores = [pltpu.make_async_copy(y, z, out_sems.at[i]) for i, (_, y, z) in enumerate(triples)]
+    for load in loads:
+        load.start()
+    for load, store in zip(loads, stores):
+        load.wait()
+        store.start()
+    for store in stores:
+        store.wait()
+
+
+def moving_params(staged):
+    return pltpu.CompilerParams(vmem_limit_bytes=2 * staged + 4 * MIB)
+
+
+def pack_spatial(kinds, arrays, slots, heads):
     frames, rows, _ = arrays[0].shape
-    others = heads - slots
-    shapes = []
-    if slots > 0:
-        shapes.append(jax.ShapeDtypeStruct((frames, 4, slots, rows, DH), BF16))
-    if others > 0:
-        shapes.append(jax.ShapeDtypeStruct((others, 2, frames, rows, DH), BF16))
+    count = len(arrays)
+    total = slots * count
 
     def kernel(kind_ref, *refs):
-        ins, outs, sems = refs[:4], refs[4:-1], refs[-1]
-        pairs = []
-        for slot in range(others):
+        ins, (out, stage, in_sems, out_sems) = refs[:count], refs[count:]
+        triples = []
+        for slot in range(slots):
             cols = head_columns(kind_ref, heads, SPATIAL, slot)
-            for place, ref in enumerate(ins[1:3]):
-                pairs.append((ref.at[:, :, cols], outs[-1].at[slot, place]))
+            for place, ref in enumerate(ins):
+                triples.append(
+                    (ref.at[:, :, cols], stage.at[slot, place], out.at[slot, place])
+                )
+        staged_copies(triples, in_sems, out_sems)
+
+    shape = (slots, count, frames, rows, DH)
+    return pl.pallas_call(
+        kernel,
+        out_shape=jax.ShapeDtypeStruct(shape, BF16),
+        in_specs=[pl.BlockSpec(memory_space=pltpu.SMEM)]
+        + [pl.BlockSpec(memory_space=pl.ANY)] * count,
+        out_specs=pl.BlockSpec(memory_space=pltpu.HBM),
+        scratch_shapes=[
+            pltpu.VMEM(shape, BF16),
+            pltpu.SemaphoreType.DMA((total,)),
+            pltpu.SemaphoreType.DMA((total,)),
+        ],
+        compiler_params=moving_params(2 * total * frames * rows * DH),
+        cost_estimate=cost(0, 4 * total * frames * rows * DH),
+        name="pack_spatial",
+    )(kinds, *arrays)
+
+
+def pack_temporal(kinds, arrays, slots, heads, after):
+    frames, rows, _ = arrays[0].shape
+    total = 4 * slots
+    extra = 0 if after is None else 1
+
+    def kernel(kind_ref, *refs):
+        ins, (out, stage, in_sems, out_sems) = refs[:4], refs[4 + extra :]
+        triples = []
         for slot in range(slots):
             cols = head_columns(kind_ref, heads, TEMPORAL, slot)
             for place, ref in enumerate(ins):
-                pairs.append((ref.at[:, :, cols], outs[0].at[:, place, slot]))
-        copy_all(pairs, sems)
-
-    outs = pl.pallas_call(
-        kernel,
-        out_shape=shapes,
-        in_specs=[pl.BlockSpec(memory_space=pltpu.SMEM)] + [pl.BlockSpec(memory_space=pl.ANY)] * 4,
-        out_specs=[pl.BlockSpec(memory_space=pl.ANY)] * len(shapes),
-        scratch_shapes=[pltpu.SemaphoreType.DMA((4 * slots + 2 * others,))],
-        compiler_params=pltpu.CompilerParams(vmem_limit_bytes=MIB),
-        cost_estimate=cost(0, 4 * (4 * slots + 2 * others) * frames * rows * DH),
-        name="pack",
-    )(kinds, *arrays)
-    return (outs[0] if slots > 0 else None), (outs[-1] if others > 0 else None)
+                triples.append(
+                    (ref.at[:, :, cols], stage.at[slot, place], out.at[:, place, slot])
+                )
+        staged_copies(triples, in_sems, out_sems)
+
+    return pl.pallas_call(
+        kernel,
+        out_shape=jax.ShapeDtypeStruct((frames, 4, slots, rows, DH), BF16),
+        in_specs=[pl.BlockSpec(memory_space=pltpu.SMEM)]
+        + [pl.BlockSpec(memory_space=pl.ANY)] * (4 + extra),
+        out_specs=pl.BlockSpec(memory_space=pltpu.HBM),
+        scratch_shapes=[
+            pltpu.VMEM((slots, 4, frames, rows, DH), BF16),
+            pltpu.SemaphoreType.DMA((total,)),
+            pltpu.SemaphoreType.DMA((total,)),
+        ],
+        compiler_params=moving_params(2 * total * frames * rows * DH),
+        cost_estimate=cost(0, 4 * total * frames * rows * DH),
+        name="pack_temporal",
+    )(kinds, *arrays, *([] if after is None else [after]))
 
 
 def temporal(kinds, bands, rows_in, heads):
@@ -103,8 +143,29 @@
     group = 16
     size = frames * group
 
-    def kernel(kind_ref, band_ref, in_ref, out_ref):
-        band = band_ref[head_at(kind_ref, heads, TEMPORAL, pl.program_id(0))]
+    def kernel(kind_ref, band_ref, rows_ref, result_ref, held, made, in_sems, out_sems):
+        def load(slot):
+            return pltpu.make_async_copy(rows_ref.at[:, :, slot], held.at[slot], in_sems.at[slot])
+
+        def store(slot):
+            return pltpu.make_async_copy(
+                made.at[slot], result_ref.at[:, :, slot], out_sems.at[slot]
+            )
+
+        for slot in range(slots):
+            load(slot).start()
+
+        @pl.loop(0, slots)
+        def _(slot):
+            load(slot).wait()
+            one_head(kind_ref, band_ref, slot, held.at[slot], made.at[slot])
+            store(slot).start()
+
+        for slot in range(slots):
+            store(slot).wait()
+
+    def one_head(kind_ref, band_ref, slot, in_ref, out_ref):
+        band = band_ref[head_at(kind_ref, heads, TEMPORAL, slot)]
         row = lax.broadcasted_iota(jnp.int32, (size, size), 0)
         col = lax.broadcasted_iota(jnp.int32, (size, size), 1)
         same = lax.rem(row, group) == lax.rem(col, group)
@@ -112,7 +173,7 @@
         allowed = jnp.logical_and(same, near)
         parts = [slice(start, start + group) for start in range(0, rows, group)]
         qs, ks, vs, gs = (
-            [in_ref[:, place, 0, part].reshape(size, DH) for part in parts] for place in range(4)
+            [in_ref[:, place, part].reshape(size, DH) for part in parts] for place in range(4)
         )
         scores = [jnp.where(allowed, dot_nt(q, k) * SCALE, MASKED) for q, k in zip(qs, ks)]
         dprobs = [dot_nt(g, v) for g, v in zip(gs, vs)]
@@ -136,18 +197,22 @@
         )
         for place, result in enumerate(results):
             for part, value in zip(parts, result):
-                out_ref[:, place, 0, part] = value.reshape(frames, group, DH)
-
-    spec = pl.BlockSpec(
-        (frames, 4, 1, rows, DH), lambda i, kind_ref, band_ref: (0, 0, i, 0, 0)
-    )
+                out_ref[:, place, part] = value.reshape(frames, group, DH)
+
+    block = (slots, frames, 4, rows, DH)
     return pl.pallas_call(
         kernel,
         out_shape=jax.ShapeDtypeStruct(rows_in.shape, BF16),
-        grid_spec=pltpu.PrefetchScalarGridSpec(
-            num_scalar_prefetch=2, grid=(slots,), in_specs=[spec], out_specs=spec
-        ),
-        compiler_params=params(),
+        in_specs=[pl.BlockSpec(memory_space=pltpu.SMEM)] * 2
+        + [pl.BlockSpec(memory_space=pl.ANY)],
+        out_specs=pl.BlockSpec(memory_space=pltpu.HBM),
+        scratch_shapes=[
+            pltpu.VMEM(block, BF16),
+            pltpu.VMEM(block, BF16),
+            pltpu.SemaphoreType.DMA((slots,)),
+            pltpu.SemaphoreType.DMA((slots,)),
+        ],
+        compiler_params=pltpu.CompilerParams(vmem_limit_bytes=48 * MIB),
         cost_estimate=cost(12 * slots * rows * frames * size * DH, 4 * rows_in.size),
         name="temporal",
     )(kinds, bands, rows_in)
@@ -157,23 +222,29 @@
     frames, _, slots, rows, _ = rows_in.shape
 
     def kernel(kind_ref, in_ref, *refs):
-        outs, sems = refs[-5:-1], refs[-1]
-        pairs = []
+        outs, (stage, in_sems, out_sems) = refs[-7:-3], refs[-3:]
+        triples = []
         for slot in range(slots):
             cols = head_columns(kind_ref, heads, TEMPORAL, slot)
             for place, ref in enumerate(outs):
-                pairs.append((in_ref.at[:, place, slot], ref.at[:, :, cols]))
-        copy_all(pairs, sems)
+                triples.append(
+                    (in_ref.at[:, place, slot], stage.at[slot, place], ref.at[:, :, cols])
+                )
+        staged_copies(triples, in_sems, out_sems)
 
     return pl.pallas_call(
         kernel,
         out_shape=[jax.ShapeDtypeStruct((frames, rows, heads * DH), BF16)] * 4,
         in_specs=[pl.BlockSpec(memory_space=pltpu.SMEM)]
         + [pl.BlockSpec(memory_space=pl.ANY)] * (1 + len(filled)),
-        out_specs=[pl.BlockSpec(memory_space=pl.ANY)] * 4,
-        scratch_shapes=[pltpu.SemaphoreType.DMA((4 * slots,))],
+        out_specs=[pl.BlockSpec(memory_space=pltpu.HBM)] * 4,
+        scratch_shapes=[
+            pltpu.VMEM((slots, 4, frames, rows, DH), BF16),
+            pltpu.SemaphoreType.DMA((4 * slots,)),
+            pltpu.SemaphoreType.DMA((4 * slots,)),
+        ],
         input_output_aliases={2 + place: place for place in range(len(filled))},
-        compiler_params=pltpu.CompilerParams(vmem_limit_bytes=MIB),
+        compiler_params=moving_params(2 * rows_in.size),
         cost_estimate=cost(0, 4 * rows_in.size),
         name="unpack",
     )(kinds, rows_in, *filled)
@@ -241,7 +312,7 @@
             in_specs=[columns] * 4 + [pair],
             out_specs=[columns, columns, pair, pair],
         ),
-        compiler_params=params(48),
+        compiler_params=params(60),
         cost_estimate=cost(24 * slots * count * count * DH, 12 * 2 * slots * count * DH),
         name="spatial",
     )(kinds, frame, *arrays, prior)
@@ -282,16 +353,17 @@
     exchange = functools.partial(
         lax.all_to_all, axis_name="ctx", split_axis=0, concat_axis=0, tiled=True
     )
-    packed, pairs = pack(kinds, (q, k, v, g), slots, heads)
-    filled = ()
+    filled, pairs = (), None
+    if slots < heads:
+        pairs = pack_spatial(kinds, (k, v), heads - slots, heads)
     if slots > 0:
-        framed = exchange(packed)
+        framed = exchange(pack_temporal(kinds, (q, k, v, g), slots, heads, pairs))
     if slots < heads:
         prior = passed_along(pairs, "ctx", 1).reshape(heads - slots, 2, count, DH)
         flat = [x.reshape(count, width) for x in (q, k, v, g)]
         attended, qgrad, own, send = spatial(kinds, frame, flat, prior, heads)
         if slots > 0:
-            framed, send = lax.optimization_barrier((framed, send))
+            framed, _ = lax.optimization_barrier((framed, send))
         back = passed_along(send, "ctx", -1)
         filled = (attended, qgrad, *add_spatial(kinds, own, back, heads))
         filled = tuple(x.reshape(q.shape) for x in filled)

time: 152 us -> 163 us (1.072); the launches traced: 152 us -> 160 us
  waiting for transfers between devices: 108 us -> 114 us
    ppermute x2, waiting for transfers between devices: 108 us -> 114 us  [passed_along(): return lax.ppermute(array, axis, pairs)]
    pallas_call x1, Pallas kernels: 7.65 us -> 5.16 us  [spatial(): pl.pallas_call(kernel, out_shape=[whole, whole, jax.ShapeDtypeStruct(prio...]
    pallas_call x1 -> x2, Pallas kernels: 2.61 us -> 4.24 us  [the longest x1 2.44 us: pack_temporal(): pl.pallas_call(kernel, out_shape=jax.ShapeDtypeStruct((frames, 4, slots,...]
    cond x6 -> x14, local copies, waits for them, and re-layouts: 3.39 us -> 3.62 us
  transfers between devices with their start and end apart: 4 -> 4, of which waited for: 2 -> 2; matrix products, arithmetic and copies ran while one was open for 0% -> 0% of each run, Pallas kernels for 6% -> 4%
where the time goes in v1:
time: 163 us; the launch traced here: 160 us
  waiting for transfers between devices  114 us (70%)
  Pallas kernels  18.7 us (11%)
  starting transfers between devices  18.6 us (11%)
  local copies, waits for them, and re-layouts  4.35 us (3%)
    ppermute x2, waiting for transfers between devices, passed_along(): return lax.ppermute(array, axis, pairs)  114 us
    all_to_all x1, starting transfers between devices, branch(): returned = exchange(temporal(kinds, bands, framed, heads))  6.23 us
    all_to_all x1, starting transfers between devices, branch(): framed = exchange(pack_temporal(kinds, (q, k, v, g), slots, heads, pairs))  6.22 us
    ppermute x2, starting transfers between devices, passed_along(): return lax.ppermute(array, axis, pairs)  6.12 us
    pallas_call x1, Pallas kernels, temporal(): pl.pallas_call(kernel, out_shape=jax.ShapeDtypeStruct(rows_in.shape, BF16...  5.18 us
    pallas_call x1, Pallas kernels, spatial(): pl.pallas_call(kernel, out_shape=[whole, whole, jax.ShapeDtypeStruct(prio...  5.16 us
    cond x14, local copies, waits for them, and re-layouts  3.62 us
  transfers between devices with their start and end apart: 4, of which 2 were waited for; matrix products, arithmetic and copies ran while one was open for 0% of the time, Pallas kernels for 4%

profile of v1, /device:TPU:14, one launch (start us, length us, event | category | flops | bytes accessed | tf_op | source)
XLA Modules:
  0.0 159.8 jit_solution(1227938112578719064)
XLA Ops:
  0.6 0.7 dynamic_slice.7
  1.4 1.4 fusion
  3.4 156.2 %conditional.1 = (bf16[1,512,768]{2,1,0:T(8,128)(2,1)}, bf16[1,512,768]{2,1,0:T(8,128)(2,1)}, bf16[1,512,768]{2,1,0:T(8,128)(2,1)}, bf16[1,512,768]{2,1,0:T(8,128)(2,1)}) conditional(s32[]{:T(128)} %clamp.3, (bf16[1,512,768]{2,1,0:T(8,128)(2,1)}, bf16[1,512,768]{2,1,0:T(8,128)(2,1)}, bf16[1,512,768]{2,1,0:T(8,128)(2,1)}, ...), branch_computations={%region_1.0_spmd, %region_2.0_spmd, %region_3.0_spmd, %region_4.0_... | conditional | flops 4831838208 | bytes 68157808 | solution.py:389
  3.6 0.0 copy-start.14
  3.7 0.0 copy-start.20
  3.7 1.8 %pack_spatial.11.refs_4_ = bf16[1,2,8,64,128]{4,3,2,1,0:T(8,128)(2,1)S(1)} custom-call(s32[6]{0:T(128)S(1)} %get-tuple-element.268.kind_ref, bf16[8,64,768]{2,1,0:T(8,128)(2,1)} %bitcast.103, bf16[8,64,768]{2,1,0:T(8,128)(2,1)} %bitcast.126), custom_call_target="tpu_custom_call" | custom-call | bytes 524288 | tf_op jit(solution)/shard_map/cond/branch_5_fun/pack_spatial/pallas_call | solution.py:91
  5.5 0.0 copy-done.14
  5.5 0.0 copy-done.20
  5.5 2.4 %pack_temporal.10 = bf16[8,4,5,64,128]{4,3,2,1,0:T(8,128)(2,1)S(1)} custom-call(s32[6]{0:T(128)S(1)} %get-tuple-element.268.kind_ref, bf16[8,64,768]{2,1,0:T(8,128)(2,1)} %bitcast.144, bf16[8,64,768]{2,1,0:T(8,128)(2,1)S(1)} %bitcast.105, bf16[8,64,768]{2,1,0:T(8,128)(2,1)S(1)} %bitcast.128, bf16[8,64,768]{2,1,0:T(8,128)(2,1)} %bitcast.161, ...), custom_call_target="tpu_custom_call" | custom-call | bytes 5242880 | tf_op jit(solution)/shard_map/cond/branch_5_fun/pack_temporal/pallas_call | solution.py:124
  7.9 0.0 copy-start
  8.0 1.4 copy-done
  9.4 6.2 %all-to-all-start.8 = ((bf16[8,4,5,64,128]{4,3,2,1,0:T(8,128)(2,1)}), bf16[8,4,5,64,128]{4,3,2,1,0:T(8,128)(2,1)S(1)}, u32[]{:S(2)}, u32[]{:S(2)}) async-start(bf16[8,4,5,64,128]{4,3,2,1,0:T(8,128)(2,1)} %copy-done), calls=%async_computation.8 | async-start | bytes 5242880 | tf_op jit(solution)/shard_map/cond/branch_5_fun/all_to_all | solution.py:360
  15.6 3.7 %collective-permute-start.10 = (bf16[1,2,8,64,128]{4,3,2,1,0:T(8,128)(2,1)S(1)}, bf16[1,2,8,64,128]{4,3,2,1,0:T(8,128)(2,1)S(1)}, u32[]{:S(2)}, u32[]{:S(2)}) collective-permute-start(bf16[1,2,8,64,128]{4,3,2,1,0:T(8,128)(2,1)S(1)} %pack_spatial.11.refs_4_), channel_id=1, source_target_pairs={{0,4},{4,8},{8,12},{12,16},{16,20},{20,24},{24,28},{1,5},{5,9},{9,... | collective-permute-start | bytes 786440 | tf_op jit(solution)/shard_map/cond/branch_5_fun/ppermute | solution.py:347
  19.3 54.8 %collective-permute-done.10 = bf16[1,2,8,64,128]{4,3,2,1,0:T(8,128)(2,1)S(1)} collective-permute-done((bf16[1,2,8,64,128]{4,3,2,1,0:T(8,128)(2,1)S(1)}, bf16[1,2,8,64,128]{4,3,2,1,0:T(8,128)(2,1)S(1)}, u32[]{:S(2)}, u32[]{:S(2)}) %collective-permute-start.10) | collective-permute-done | bytes 262176 | tf_op jit(solution)/shard_map/cond/branch_5_fun/ppermute | solution.py:347
  74.1 0.0 copy-start.30
  74.1 0.7 copy-done.30
  74.8 5.2 %spatial.11 = (bf16[512,768]{1,0:T(8,128)(2,1)}, bf16[512,768]{1,0:T(8,128)(2,1)}, f32[1,2,512,128]{3,2,1,0:T(8,128)}, bf16[1,2,512,128]{3,2,1,0:T(8,128)(2,1)}) custom-call(s32[6]{0:T(128)S(1)} %get-tuple-element.268.kind_ref, s32[1]{0:T(128)} %get-tuple-element.274.frame_ref, bf16[512,768]{1,0:T(8,128)(2,1)} %bitcast.145, bf16[512,768]{1,0:T(8,128)(2,1)} %bitcast.104, ...), custom_call_target="tpu_custom_call" | custom-call | flops 805306368 | bytes 1572864 | tf_op jit(solution)/shard_map/cond/branch_5_fun/spatial/pallas_call | solution.py:301
  80.0 0.0 all-to-all-done.8.rows_ref
  80.0 5.2 %temporal.10 = bf16[8,4,5,64,128]{4,3,2,1,0:T(8,128)(2,1)S(1)} custom-call(s32[6]{0:T(128)S(1)} %get-tuple-element.268.kind_ref, s32[6]{0:T(128)S(1)} %get-tuple-element.269.band_ref, bf16[8,4,5,64,128]{4,3,2,1,0:T(8,128)(2,1)S(1)} %all-to-all-done.8.rows_ref), custom_call_target="tpu_custom_call" | custom-call | flops 503316480 | bytes 5242880 | tf_op jit(solution)/shard_map/cond/branch_5_fun/temporal/pallas_call | solution.py:203
  85.1 0.0 copy-start.1
  85.2 1.4 copy-done.1
  86.6 0.0 copy-start.35
  86.6 0.0 copy-start.8
  86.6 6.2 %all-to-all-start.9 = ((bf16[8,4,5,64,128]{4,3,2,1,0:T(8,128)(2,1)}), bf16[8,4,5,64,128]{4,3,2,1,0:T(8,128)(2,1)S(1)}, u32[]{:S(2)}, u32[]{:S(2)}) async-start(bf16[8,4,5,64,128]{4,3,2,1,0:T(8,128)(2,1)} %copy-done.1), calls=%async_computation.9 | async-start | bytes 5242880 | tf_op jit(solution)/shard_map/cond/branch_5_fun/all_to_all | solution.py:371
  92.8 0.0 copy-done.35
  92.8 2.5 %collective-permute-start.11 = (bf16[1,2,512,128]{3,2,1,0:T(8,128)(2,1)S(1)}, bf16[1,2,512,128]{3,2,1,0:T(8,128)(2,1)S(1)}, u32[]{:S(2)}, u32[]{:S(2)}) collective-permute-start(bf16[1,2,512,128]{3,2,1,0:T(8,128)(2,1)S(1)} %copy-done.35), channel_id=1, source_target_pairs={{4,0},{8,4},{12,8},{16,12},{20,16},{24,20},{28,24},{5,1},{9,5},{13... | collective-permute-start | bytes 786440 | tf_op jit(solution)/shard_map/cond/branch_5_fun/ppermute | solution.py:347
  95.3 59.6 %collective-permute-done.11.back_ref = bf16[1,2,512,128]{3,2,1,0:T(8,128)(2,1)S(1)} collective-permute-done((bf16[1,2,512,128]{3,2,1,0:T(8,128)(2,1)S(1)}, bf16[1,2,512,128]{3,2,1,0:T(8,128)(2,1)S(1)}, u32[]{:S(2)}, u32[]{:S(2)}) %collective-permute-start.11) | collective-permute-done | bytes 262176 | tf_op jit(solution)/shard_map/cond/branch_5_fun/ppermute | solution.py:347
  154.9 0.0 copy-done.8
  154.9 1.3 add_spatial.11
  156.2 0.0 all-to-all-done.9.in_ref
  156.2 2.8 %unpack.10 = (bf16[8,64,768]{2,1,0:T(8,128)(2,1)}, bf16[8,64,768]{2,1,0:T(8,128)(2,1)}, bf16[8,64,768]{2,1,0:T(8,128)(2,1)}, bf16[8,64,768]{2,1,0:T(8,128)(2,1)}) custom-call(s32[6]{0:T(128)S(1)} %get-tuple-element.268.kind_ref, ...), custom_call_target="tpu_custom_call", output_to_operand_aliasing={{0}: (2, {}), {1}: (3, {}), {2}: (4, {}), {3}: (5, {})} | custom-call | bytes 5242880 | tf_op jit(solution)/shard_map/cond/branch_5_fun/unpack/pallas_call | solution.py:235
Async XLA Ops:
  3.6 1.8 %copy-start.14 = (bf16[1,512,768]{2,1,0:T(8,128)(2,1)S(1)}, bf16[1,512,768]{2,1,0:T(8,128)(2,1)}, u32[]{:S(2)}) copy-start(bf16[1,512,768]{2,1,0:T(8,128)(2,1)} %get-tuple-element.276) | copy-start | bytes 2359300 | tf_op jit(solution)/shard_map/cond
  3.7 1.8 %copy-start.20 = (bf16[1,512,768]{2,1,0:T(8,128)(2,1)S(1)}, bf16[1,512,768]{2,1,0:T(8,128)(2,1)}, u32[]{:S(2)}) copy-start(bf16[1,512,768]{2,1,0:T(8,128)(2,1)} %get-tuple-element.277) | copy-start | bytes 2359300 | tf_op jit(solution)/shard_map/cond
  7.9 1.5 copy-start
  9.4 70.6 %all-to-all-start.8 = ((bf16[8,4,5,64,128]{4,3,2,1,0:T(8,128)(2,1)}), bf16[8,4,5,64,128]{4,3,2,1,0:T(8,128)(2,1)S(1)}, u32[]{:S(2)}, u32[]{:S(2)}) async-start(bf16[8,4,5,64,128]{4,3,2,1,0:T(8,128)(2,1)} %copy-done), calls=%async_computation.8 | async-start | bytes 5242880 | tf_op jit(solution)/shard_map/cond/branch_5_fun/all_to_all | solution.py:360
  15.6 58.5 %collective-permute-start.10 = (bf16[1,2,8,64,128]{4,3,2,1,0:T(8,128)(2,1)S(1)}, bf16[1,2,8,64,128]{4,3,2,1,0:T(8,128)(2,1)S(1)}, u32[]{:S(2)}, u32[]{:S(2)}) collective-permute-start(bf16[1,2,8,64,128]{4,3,2,1,0:T(8,128)(2,1)S(1)} %pack_spatial.11.refs_4_), channel_id=1, source_target_pairs={{0,4},{4,8},{8,12},{12,16},{16,20},{20,24},{24,28},{1,5},{5,9},{9,... | collective-permute-start | bytes 786440 | tf_op jit(solution)/shard_map/cond/branch_5_fun/ppermute | solution.py:347
  74.1 0.7 copy-start.30
  85.1 1.5 copy-start.1
  86.6 6.2 %copy-start.35 = (bf16[1,2,512,128]{3,2,1,0:T(8,128)(2,1)S(1)}, bf16[1,2,512,128]{3,2,1,0:T(8,128)(2,1)}, u32[]{:S(2)}) copy-start(bf16[1,2,512,128]{3,2,1,0:T(8,128)(2,1)} %get-tuple-element.279) | copy-start | bytes 786436 | tf_op jit(solution)/shard_map/cond
  86.6 68.3 %copy-start.8 = (f32[1,2,512,128]{3,2,1,0:T(8,128)S(1)}, f32[1,2,512,128]{3,2,1,0:T(8,128)}, u32[]{:S(2)}) copy-start(f32[1,2,512,128]{3,2,1,0:T(8,128)} %get-tuple-element.283.own_ref) | copy-start | bytes 1572868 | tf_op jit(solution)/shard_map/cond
  86.6 69.5 %all-to-all-start.9 = ((bf16[8,4,5,64,128]{4,3,2,1,0:T(8,128)(2,1)}), bf16[8,4,5,64,128]{4,3,2,1,0:T(8,128)(2,1)S(1)}, u32[]{:S(2)}, u32[]{:S(2)}) async-start(bf16[8,4,5,64,128]{4,3,2,1,0:T(8,128)(2,1)} %copy-done.1), calls=%async_computation.9 | async-start | bytes 5242880 | tf_op jit(solution)/shard_map/cond/branch_5_fun/all_to_all | solution.py:371
  92.8 62.0 %collective-permute-start.11 = (bf16[1,2,512,128]{3,2,1,0:T(8,128)(2,1)S(1)}, bf16[1,2,512,128]{3,2,1,0:T(8,128)(2,1)S(1)}, u32[]{:S(2)}, u32[]{:S(2)}) collective-permute-start(bf16[1,2,512,128]{3,2,1,0:T(8,128)(2,1)S(1)} %copy-done.35), channel_id=1, source_target_pairs={{4,0},{8,4},{12,8},{16,12},{20,16},{24,20},{28,24},{5,1},{9,5},{13... | collective-permute-start | bytes 786440 | tf_op jit(solution)/shard_map/cond/branch_5_fun/ppermute | solution.py:347

commit v2 on v1

v2 whole, which is shorter than its diff:
```python
import functools

import jax
import jax.numpy as jnp
from jax import lax
from jax.experimental import pallas as pl
from jax.experimental.pallas import tpu as pltpu
from jax.sharding import PartitionSpec as P

DH = 128
SCALE = DH ** (-0.5)
SPATIAL, TEMPORAL = 1, 0
MASKED = -1e30
F32 = jnp.float32
BF16 = jnp.bfloat16
MIB = 1024 * 1024


def head_at(kind_ref, first_ref, heads, kind, slot):
    found, seen = jnp.int32(0), jnp.int32(0)
    for head in range(heads):
        hit = kind_ref[first_ref[0] + head] == kind
        found = jnp.where(jnp.logical_and(hit, seen == slot), jnp.int32(head), found)
        seen = seen + hit.astype(jnp.int32)
    return found


def dot_nt(a, b):
    return lax.dot_general(a, b, (((1,), (1,)), ((), ())), preferred_element_type=F32)


def dot_nn(a, b):
    return lax.dot_general(a, b, (((1,), (0,)), ((), ())), preferred_element_type=F32)


def dot_tn(a, b):
    return lax.dot_general(a, b, (((0,), (0,)), ((), ())), preferred_element_type=F32)


def params(mib=32):
    return pltpu.CompilerParams(
        dimension_semantics=("arbitrary",), vmem_limit_bytes=mib * MIB
    )


def cost(flops, moved):
    return pl.CostEstimate(flops=int(flops), bytes_accessed=int(moved), transcendentals=0)


def column_spec(count, heads, kind):
    return pl.BlockSpec((count, DH), lambda i, *refs: (0, head_at(*refs[:2], heads, kind, i)))


def head_columns(kind_ref, first_ref, heads, kind, slot):
    return pl.ds(pl.multiple_of(head_at(kind_ref, first_ref, heads, kind, slot) * DH, DH), DH)


def staged_copies(triples, in_sems, out_sems):
    loads = [pltpu.make_async_copy(x, y, in_sems.at[i]) for i, (x, y, _) in enumerate(triples)]
    stores = [pltpu.make_async_copy(y, z, out_sems.at[i]) for i, (_, y, z) in enumerate(triples)]
    for load in loads:
        load.start()
    for load, store in zip(loads, stores):
        load.wait()
        store.start()
    for store in stores:
        store.wait()


def whole_params():
    return pltpu.CompilerParams(vmem_limit_bytes=62 * MIB)


def pack_spatial(kinds, first, arrays, slots, heads):
    frames, rows, _ = arrays[0].shape
    count = len(arrays)
    total = slots * count

    def kernel(kind_ref, first_ref, *refs):
        ins, outs = refs[:count], refs[count:-3]
        stage, in_sems, out_sems = refs[-3:]
        triples = []
        for slot in range(slots):
            cols = head_columns(kind_ref, first_ref, heads, SPATIAL, slot)
            for place, ref in enumerate(ins):
                target = outs[place // 2].at[slot, place % 2]
                triples.append((ref.at[:, :, cols], stage.at[slot, place], target))
        staged_copies(triples, in_sems, out_sems)

    pair = jax.ShapeDtypeStruct((slots, 2, frames, rows, DH), BF16)
    return pl.pallas_call(
        kernel,
        out_shape=[pair] * (count // 2),
        in_specs=[pl.BlockSpec(memory_space=pltpu.SMEM)] * 2
        + [pl.BlockSpec(memory_space=pl.ANY)] * count,
        out_specs=[pl.BlockSpec(memory_space=pl.ANY)] * (count // 2),
        scratch_shapes=[
            pltpu.VMEM((slots, count, frames, rows, DH), BF16),
            pltpu.SemaphoreType.DMA((total,)),
            pltpu.SemaphoreType.DMA((total,)),
        ],
        compiler_params=whole_params(),
        cost_estimate=cost(0, 4 * total * frames * rows * DH),
        name="pack_spatial",
    )(kinds, first, *arrays)


def pack_temporal(kinds, first, arrays, slots, heads):
    frames, rows, _ = arrays[0].shape
    total = 4 * slots

    def kernel(kind_ref, first_ref, *refs):
        ins, (out, stage, in_sems, out_sems) = refs[:4], refs[4:]
        triples = []
        for slot in range(slots):
            cols = head_columns(kind_ref, first_ref, heads, TEMPORAL, slot)
            for place, ref in enumerate(ins):
                triples.append(
                    (ref.at[:, :, cols], stage.at[slot, place], out.at[:, place, slot])
                )
        staged_copies(triples, in_sems, out_sems)

    return pl.pallas_call(
        kernel,
        out_shape=jax.ShapeDtypeStruct((frames, 4, slots, rows, DH), BF16),
        in_specs=[pl.BlockSpec(memory_space=pltpu.SMEM)] * 2
        + [pl.BlockSpec(memory_space=pl.ANY)] * 4,
        out_specs=pl.BlockSpec(memory_space=pl.ANY),
        scratch_shapes=[
            pltpu.VMEM((slots, 4, frames, rows, DH), BF16),
            pltpu.SemaphoreType.DMA((total,)),
            pltpu.SemaphoreType.DMA((total,)),
        ],
        compiler_params=whole_params(),
        cost_estimate=cost(0, 4 * total * frames * rows * DH),
        name="pack_temporal",
    )(kinds, first, *arrays)


def temporal(kinds, first, bands, rows_in, heads):
    frames, _, slots, rows, _ = rows_in.shape
    group = 16
    size = frames * group

    def kernel(kind_ref, first_ref, band_ref, rows_ref, result_ref, held, made, in_sems, out_sems):
        def load(slot):
            return pltpu.make_async_copy(rows_ref.at[:, :, slot], held.at[slot], in_sems.at[slot])

        def store(slot):
            return pltpu.make_async_copy(
                made.at[slot], result_ref.at[:, :, slot], out_sems.at[slot]
            )

        for slot in range(slots):
            load(slot).start()

        @pl.loop(0, slots)
        def _(slot):
            load(slot).wait()
            one_head(kind_ref, first_ref, band_ref, slot, held.at[slot], made.at[slot])
            store(slot).start()

        for slot in range(slots):
            store(slot).wait()

    def one_head(kind_ref, first_ref, band_ref, slot, in_ref, out_ref):
        band = band_ref[first_ref[0] + head_at(kind_ref, first_ref, heads, TEMPORAL, slot)]
        row = lax.broadcasted_iota(jnp.int32, (size, size), 0)
        col = lax.broadcasted_iota(jnp.int32, (size, size), 1)
        same = lax.rem(row, group) == lax.rem(col, group)
        near = jnp.abs(lax.div(row, group) - lax.div(col, group)) <= band
        allowed = jnp.logical_and(same, near)
        parts = [slice(start, start + group) for start in range(0, rows, group)]
        qs, ks, vs, gs = (
            [in_ref[:, place, part].reshape(size, DH) for part in parts] for place in range(4)
        )
        scores = [jnp.where(allowed, dot_nt(q, k) * SCALE, MASKED) for q, k in zip(qs, ks)]
        dprobs = [dot_nt(g, v) for g, v in zip(gs, vs)]
        raised = [jnp.exp(x - jnp.max(x, axis=1, keepdims=True)) for x in scores]
        weights = [x * (1.0 / jnp.sum(x, axis=1, keepdims=True)) for x in raised]
        probs = [x.astype(BF16) for x in weights]
        attended = [dot_nn(x, v).astype(BF16) for x, v in zip(probs, vs)]
        deltas = [
            jnp.sum(g.astype(F32) * x.astype(F32), axis=1, keepdims=True)
            for g, x in zip(gs, attended)
        ]
        dscores = [
            (w * (dp - delta) * SCALE).astype(BF16)
            for w, dp, delta in zip(weights, dprobs, deltas)
        ]
        results = (
            attended,
            [dot_nn(x, k).astype(BF16) for x, k in zip(dscores, ks)],
            [dot_tn(x, q).astype(BF16) for x, q in zip(dscores, qs)],
            [dot_tn(x, g).astype(BF16) for x, g in zip(probs, gs)],
        )
        for place, result in enumerate(results):
            for part, value in zip(parts, result):
                out_ref[:, place, part] = value.reshape(frames, group, DH)

    block = (slots, frames, 4, rows, DH)
    return pl.pallas_call(
        kernel,
        out_shape=jax.ShapeDtypeStruct(rows_in.shape, BF16),
        in_specs=[pl.BlockSpec(memory_space=pltpu.SMEM)] * 3
        + [pl.BlockSpec(memory_space=pl.ANY)],
        out_specs=pl.BlockSpec(memory_space=pl.ANY),
        scratch_shapes=[
            pltpu.VMEM(block, BF16),
            pltpu.VMEM(block, BF16),
            pltpu.SemaphoreType.DMA((slots,)),
            pltpu.SemaphoreType.DMA((slots,)),
        ],
        compiler_params=whole_params(),
        cost_estimate=cost(12 * slots * rows * frames * size * DH, 4 * rows_in.size),
        name="temporal",
    )(kinds, first, bands, rows_in)


def unpack(kinds, first, rows_in, filled, heads):
    frames, _, slots, rows, _ = rows_in.shape

    def kernel(kind_ref, first_ref, in_ref, *refs):
        outs, (stage, in_sems, out_sems) = refs[-7:-3], refs[-3:]
        triples = []
        for slot in range(slots):
            cols = head_columns(kind_ref, first_ref, heads, TEMPORAL, slot)
            for place, ref in enumerate(outs):
                triples.append(
                    (in_ref.at[:, place, slot], stage.at[slot, place], ref.at[:, :, cols])
                )
        staged_copies(triples, in_sems, out_sems)

    return pl.pallas_call(
        kernel,
        out_shape=[jax.ShapeDtypeStruct((frames, rows, heads * DH), BF16)] * 4,
        in_specs=[pl.BlockSpec(memory_space=pltpu.SMEM)] * 2
        + [pl.BlockSpec(memory_space=pl.ANY)] * (1 + len(filled)),
        out_specs=[pl.BlockSpec(memory_space=pl.ANY)] * 4,
        scratch_shapes=[
            pltpu.VMEM((slots, 4, frames, rows, DH), BF16),
            pltpu.SemaphoreType.DMA((4 * slots,)),
            pltpu.SemaphoreType.DMA((4 * slots,)),
        ],
        input_output_aliases={3 + place: place for place in range(len(filled))},
        compiler_params=whole_params(),
        cost_estimate=cost(0, 4 * rows_in.size),
        name="unpack",
    )(kinds, first, rows_in, *filled)


def spatial(kinds, first, frame, arrays, prior, heads):
    count = arrays[0].shape[0]
    slots = prior.shape[0]
    chunk = min(count, 256)

    def kernel(
        kind_ref, first_ref, frame_ref, q_ref, k_ref, v_ref, g_ref, prior_ref,
        out_ref, qgrad_ref, own_ref, stats_ref,
    ):
        has_prior = frame_ref[0] > 0
        k, v = k_ref[...], v_ref[...]
        k_prior, v_prior = prior_ref[0, 0], prior_ref[0, 1]
        k_own = v_own = None
        for start in range(0, count, chunk):
            part = slice(start, start + chunk)
            q, g = q_ref[part], g_ref[part]
            own = dot_nt(q, k) * SCALE
            before = jnp.where(has_prior, dot_nt(q, k_prior) * SCALE, MASKED)
            top = jnp.maximum(
                jnp.max(own, axis=1, keepdims=True), jnp.max(before, axis=1, keepdims=True)
            )
            own, before = jnp.exp(own - top), jnp.exp(before - top)
            total = jnp.sum(own, axis=1, keepdims=True) + jnp.sum(before, axis=1, keepdims=True)
            inverse = 1.0 / total
            own, before = own * inverse, before * inverse
            own_prob, before_prob = own.astype(BF16), before.astype(BF16)
            attended = (dot_nn(own_prob, v) + dot_nn(before_prob, v_prior)).astype(BF16)
            delta = jnp.sum(g.astype(F32) * attended.astype(F32), axis=1, keepdims=True)
            own_ds = (own * (dot_nt(g, v) - delta) * SCALE).astype(BF16)
            before_ds = (before * (dot_nt(g, v_prior) - delta) * SCALE).astype(BF16)
            out_ref[part] = attended
            qgrad_ref[part] = (dot_nn(own_ds, k) + dot_nn(before_ds, k_prior)).astype(BF16)
            k_term, v_term = dot_tn(own_ds, q), dot_tn(own_prob, g)
            k_own = k_term if start == 0 else k_own + k_term
            v_own = v_term if start == 0 else v_own + v_term
            lane = lax.broadcasted_iota(jnp.int32, (chunk, DH), 1)
            stats = jnp.where(lane == 0, top + jnp.log(total), delta)
            stats_ref[0, :, part] = stats.T[:2]
        own_ref[0, 0], own_ref[0, 1] = k_own, v_own

    columns = column_spec(count, heads, SPATIAL)
    pair = pl.BlockSpec((1, 2, count, DH), lambda i, *refs: (i, 0, 0, 0))
    whole = jax.ShapeDtypeStruct((count, heads * DH), BF16)
    return pl.pallas_call(
        kernel,
        out_shape=[
            whole,
            whole,
            jax.ShapeDtypeStruct(prior.shape, F32),
            jax.ShapeDtypeStruct((slots, 2, count), F32),
        ],
        grid_spec=pltpu.PrefetchScalarGridSpec(
            num_scalar_prefetch=3,
            grid=(slots,),
            in_specs=[columns] * 4 + [pair],
            out_specs=[
                columns, columns, pair, pl.BlockSpec((1, 2, count), lambda i, *refs: (i, 0, 0))
            ],
        ),
        compiler_params=params(60),
        cost_estimate=cost(20 * slots * count * count * DH, 16 * slots * count * DH),
        name="spatial",
    )(kinds, first, frame, *arrays, prior)


def spatial_next(kinds, first, k, v, following, stats, own, heads):
    slots, _, count, _ = own.shape
    chunk = min(count, 256)

    def kernel(
        kind_ref, first_ref, k_ref, v_ref, next_ref, stats_ref, own_ref, kgrad_ref, vgrad_ref
    ):
        q, g = next_ref[0, 0], next_ref[0, 1]
        lse, delta = stats_ref[0, 0:1], stats_ref[0, 1:2]
        for start in range(0, count, chunk):
            part = slice(start, start + chunk)
            weight = jnp.exp(dot_nt(k_ref[part], q) * SCALE - lse)
            dscore = (weight * (dot_nt(v_ref[part], g) - delta) * SCALE).astype(BF16)
            kgrad_ref[part] = (own_ref[0, 0, part] + dot_nn(dscore, q)).astype(BF16)
            vgrad_ref[part] = (own_ref[0, 1, part] + dot_nn(weight.astype(BF16), g)).astype(BF16)

    columns = column_spec(count, heads, SPATIAL)
    pair = pl.BlockSpec((1, 2, count, DH), lambda i, *refs: (i, 0, 0, 0))
    return pl.pallas_call(
        kernel,
        out_shape=[jax.ShapeDtypeStruct((count, heads * DH), BF16)] * 2,
        grid_spec=pltpu.PrefetchScalarGridSpec(
            num_scalar_prefetch=2,
            grid=(slots,),
            in_specs=[columns, columns, pair]
            + [pl.BlockSpec((1, 2, count), lambda i, *refs: (i, 0, 0)), pair],
            out_specs=[columns] * 2,
        ),
        compiler_params=params(60),
        cost_estimate=cost(8 * slots * count * count * DH, 20 * slots * count * DH),
        name="spatial_next",
    )(kinds, first, k, v, following, stats, own)


def passed_along(array, axis, by):
    length = lax.axis_size(axis)
    pairs = [(i, i + by) for i in range(length) if 0 <= i + by < length]
    return lax.ppermute(array, axis, pairs)


def branch(slots, heads, kinds, bands, first, frame, q, k, v, g):
    frames, rows, width = q.shape
    count = frames * rows
    others = heads - slots
    exchange = functools.partial(
        lax.all_to_all, axis_name="ctx", split_axis=0, concat_axis=0, tiled=True
    )
    filled = ()
    if slots > 0:
        framed = exchange(pack_temporal(kinds, first, (q, k, v, g), slots, heads))
    if others > 0:
        ahead, back = pack_spatial(kinds, first, (k, v, q, g), others, heads)
        if slots > 0:
            framed, ahead, back = lax.optimization_barrier((framed, ahead, back))
        prior, following = passed_along(ahead, "ctx", 1), passed_along(back, "ctx", -1)
    if slots > 0:
        results = temporal(kinds, first, bands, framed, heads)
        if others > 0:
            results, prior, following = lax.optimization_barrier((results, prior, following))
        returned = exchange(results)
    if others > 0:
        prior, following = (x.reshape(others, 2, count, DH) for x in (prior, following))
        flat = [x.reshape(count, width) for x in (q, k, v, g)]
        attended, qgrad, own, stats = spatial(kinds, first, frame, flat, prior, heads)
        stats = passed_along(stats, "ctx", -1)
        grads = spatial_next(kinds, first, flat[1], flat[2], following, stats, own, heads)
        filled = tuple(x.reshape(q.shape) for x in (attended, qgrad, *grads))
    if slots > 0:
        filled = unpack(kinds, first, returned, filled, heads)
    return tuple(filled)


def body(queries, key_rows, value_rows, out_grad, head_kind, frame_band):
    frames = lax.axis_size("ctx")
    count = queries.shape[1]
    heads = queries.shape[2] // DH
    first = lax.axis_index("head").astype(jnp.int32) * heads
    frame = lax.axis_index("ctx").astype(jnp.int32)
    kinds = lax.dynamic_slice_in_dim(head_kind, first, heads)
    slots = jnp.sum((kinds == TEMPORAL).astype(jnp.int32))
    arrays = [
        x.reshape(frames, count // frames, heads * DH)
        for x in (queries, key_rows, value_rows, out_grad)
    ]
    outs = lax.switch(
        slots,
        [functools.partial(branch, n, heads) for n in range(heads + 1)],
        head_kind, frame_band, first.reshape(1), frame.reshape(1), *arrays,
    )
    return tuple(out.reshape(queries.shape) for out in outs)


def solution(mesh):
    rows = P("ctx", None, "head")
    return jax.shard_map(
        body,
        mesh=mesh,
        in_specs=(rows, rows, rows, rows, P(), P()),
        out_specs=(rows, rows, rows, rows),
        check_vma=False,
    )
```

time: 163 us -> 150 us (0.920); the launches traced: 160 us -> 151 us
  waiting for transfers between devices: 114 us -> 98.3 us
  Pallas kernels: 18.7 us -> 27 us
  local copies, waits for them, and re-layouts: 4.35 us -> 0.63 us
  starting transfers between devices: 18.6 us -> 21.7 us
    ppermute x2 -> x3, waiting for transfers between devices: 114 us -> 52.8 us  [passed_along(): return lax.ppermute(array, axis, pairs)]
    all_to_all x2, waiting for transfers between devices: 0.01 us -> 45.5 us  [the longest x1 45.5 us: branch(): framed = exchange(pack_temporal(kinds, first, (q, k, v, g), slots, heads))]
    pallas_call x2, Pallas kernels: 3.07 us -> 7.06 us  [the longest x1 4.42 us: spatial_next(): pl.pallas_call(kernel, out_shape=[jax.ShapeDtypeStruct((count, heads * DH...]
    cond x14 -> x12, local copies, waits for them, and re-layouts: 3.62 us -> 0.63 us
    ppermute x2 -> x3, starting transfers between devices: 6.12 us -> 8.74 us  [passed_along(): return lax.ppermute(array, axis, pairs)]
    pallas_call x1, Pallas kernels: 5.16 us -> 7.67 us  [spatial(): pl.pallas_call(kernel, out_shape=[whole, whole, jax.ShapeDtypeStruct(prio...]
  transfers between devices with their start and end apart: 4 -> 5, of which waited for: 2 -> 4; matrix products, arithmetic and copies ran while one was open for 0% -> 0% of each run, Pallas kernels for 4% -> 14%
where the time goes in v2:
time: 150 us; the launch traced here: 151 us
  waiting for transfers between devices  98.3 us (66%)
  Pallas kernels  27 us (18%)
  starting transfers between devices  21.7 us (14%)
  between operations  1.51 us (1%)
    ppermute x3, waiting for transfers between devices, passed_along(): return lax.ppermute(array, axis, pairs)  52.8 us
    all_to_all x1, waiting for transfers between devices, branch(): framed = exchange(pack_temporal(kinds, first, (q, k, v, g), slots, heads))  45.5 us
    ppermute x3, starting transfers between devices, passed_along(): return lax.ppermute(array, axis, pairs)  8.74 us
    pallas_call x1, Pallas kernels, spatial(): pl.pallas_call(kernel, out_shape=[whole, whole, jax.ShapeDtypeStruct(prio...  7.67 us
    all_to_all x1, starting transfers between devices, branch(): returned = exchange(results)  6.56 us
    all_to_all x1, starting transfers between devices, branch(): framed = exchange(pack_temporal(kinds, first, (q, k, v, g), slots, heads))  6.37 us
    pallas_call x1, Pallas kernels, temporal(): pl.pallas_call(kernel, out_shape=jax.ShapeDtypeStruct(rows_in.shape, BF16...  5.85 us
    pallas_call x1, Pallas kernels, spatial_next(): pl.pallas_call(kernel, out_shape=[jax.ShapeDtypeStruct((count, heads * DH...  4.42 us
  transfers between devices with their start and end apart: 5, of which 4 were waited for; matrix products, arithmetic and copies ran while one was open for 0% of the time, Pallas kernels for 14%

profile of v2, /device:TPU:14, one launch (start us, length us, event | category | flops | bytes accessed | tf_op | source)
XLA Modules:
  0.0 151.1 jit_solution(9857633130241207213)
XLA Ops:
  0.6 1.4 fusion
  2.7 148.3 %conditional.1 = (bf16[1,512,768]{2,1,0:T(8,128)(2,1)}, bf16[1,512,768]{2,1,0:T(8,128)(2,1)}, bf16[1,512,768]{2,1,0:T(8,128)(2,1)}, bf16[1,512,768]{2,1,0:T(8,128)(2,1)}) conditional(s32[]{:T(128)} %clamp.3, (bf16[1,512,768]{2,1,0:T(8,128)(2,1)}, bf16[1,512,768]{2,1,0:T(8,128)(2,1)}, bf16[1,512,768]{2,1,0:T(8,128)(2,1)}, ...), branch_computations={%region_1.0_spmd, %region_2.0_spmd, %region_3.0_spmd, %region_4.0_... | conditional | flops 5637144576 | bytes 47482012 | solution.py:401
  2.9 3.3 %pack_temporal.9 = bf16[8,4,4,64,128]{4,3,2,1,0:T(8,128)(2,1)} custom-call(s32[24]{0:T(128)} %get-tuple-element.293.kind_ref, s32[1]{0:T(128)} %get-tuple-element.294.first_ref, bf16[8,64,768]{2,1,0:T(8,128)(2,1)} %bitcast.165, bf16[8,64,768]{2,1,0:T(8,128)(2,1)} %bitcast.111, bf16[8,64,768]{2,1,0:T(8,128)(2,1)} %bitcast.140, bf16[8,64,768]{2,1,0:T(8,128)(2,1)} %bitcast.188), custom_call_target="tpu_custom_call" | custom-call | bytes 4194304 | tf_op jit(solution)/shard_map/cond/branch_4_fun/pack_temporal/pallas_call | solution.py:123
  6.2 0.0 copy-start.4
  6.3 0.0 copy-start.10
  6.3 0.0 copy-start.21
  6.3 6.4 %all-to-all-start.6 = ((bf16[8,4,4,64,128]{4,3,2,1,0:T(8,128)(2,1)}), bf16[8,4,4,64,128]{4,3,2,1,0:T(8,128)(2,1)}, u32[]{:S(2)}, u32[]{:S(2)}) async-start(bf16[8,4,4,64,128]{4,3,2,1,0:T(8,128)(2,1)} %pack_temporal.9), calls=%async_computation.6 | async-start | bytes 4194304 | tf_op jit(solution)/shard_map/cond/branch_4_fun/all_to_all | solution.py:366
  12.6 0.0 copy-done.4
  12.6 0.0 copy-done.10
  12.7 0.0 copy-done.21
  12.7 0.0 copy-start.30
  12.7 2.6 %pack_spatial.10 = (bf16[2,2,8,64,128]{4,3,2,1,0:T(8,128)(2,1)}, bf16[2,2,8,64,128]{4,3,2,1,0:T(8,128)(2,1)}) custom-call(s32[24]{0:T(128)S(1)} %copy-done.21, s32[1]{0:T(128)} %get-tuple-element.294.first_ref, bf16[8,64,768]{2,1,0:T(8,128)(2,1)S(1)} %bitcast.112, bf16[8,64,768]{2,1,0:T(8,128)(2,1)S(1)} %bitcast.141, bf16[8,64,768]{2,1,0:T(8,128)(2,1)} %bitcast.166, ...), custom_call_target="tpu_custom_call" | custom-call | bytes 2097152 | tf_op jit(solution)/shard_map/cond/branch_4_fun/pack_spatial/pallas_call | solution.py:91
  15.3 45.5 %all-to-all-done.6.rows_ref = bf16[8,4,4,64,128]{4,3,2,1,0:T(8,128)(2,1)} async-done(((bf16[8,4,4,64,128]{4,3,2,1,0:T(8,128)(2,1)}), bf16[8,4,4,64,128]{4,3,2,1,0:T(8,128)(2,1)}, u32[]{:S(2)}, u32[]{:S(2)}) %all-to-all-start.6) | async-done | bytes 2097184 | tf_op jit(solution)/shard_map/cond/branch_4_fun/all_to_all | solution.py:366
  60.8 4.4 %collective-permute-start.12 = (bf16[2,2,8,64,128]{4,3,2,1,0:T(8,128)(2,1)}, bf16[2,2,8,64,128]{4,3,2,1,0:T(8,128)(2,1)}, u32[]{:S(2)}, u32[]{:S(2)}) collective-permute-start(bf16[2,2,8,64,128]{4,3,2,1,0:T(8,128)(2,1)} %get-tuple-element.303), channel_id=1, source_target_pairs={{0,4},{4,8},{8,12},{12,16},{16,20},{20,24},{24,28},{1,5},{5,9},{9,... | collective-permute-start | bytes 1572872 | tf_op jit(solution)/shard_map/cond/branch_4_fun/ppermute | solution.py:354
  65.2 1.9 %collective-permute-start.13 = (bf16[2,2,8,64,128]{4,3,2,1,0:T(8,128)(2,1)}, bf16[2,2,8,64,128]{4,3,2,1,0:T(8,128)(2,1)}, u32[]{:S(2)}, u32[]{:S(2)}) collective-permute-start(bf16[2,2,8,64,128]{4,3,2,1,0:T(8,128)(2,1)} %get-tuple-element.304), channel_id=1, source_target_pairs={{4,0},{8,4},{12,8},{16,12},{20,16},{24,20},{28,24},{5,1},{9,5},{13... | collective-permute-start | bytes 1572872 | tf_op jit(solution)/shard_map/cond/branch_4_fun/ppermute | solution.py:354
  67.1 0.0 copy-done.30
  67.1 5.8 %temporal.9 = bf16[8,4,4,64,128]{4,3,2,1,0:T(8,128)(2,1)} custom-call(s32[24]{0:T(128)S(1)} %copy-done.21, s32[1]{0:T(128)} %get-tuple-element.294.first_ref, s32[24]{0:T(128)S(1)} %copy-done.30, bf16[8,4,4,64,128]{4,3,2,1,0:T(8,128)(2,1)} %all-to-all-done.6.rows_ref), custom_call_target="tpu_custom_call" | custom-call | flops 402653184 | bytes 4194304 | tf_op jit(solution)/shard_map/cond/branch_4_fun/temporal/pallas_call | solution.py:202
  73.0 0.0 copy-start.14
  73.0 10.4 %collective-permute-done.12 = bf16[2,2,8,64,128]{4,3,2,1,0:T(8,128)(2,1)} collective-permute-done((bf16[2,2,8,64,128]{4,3,2,1,0:T(8,128)(2,1)}, bf16[2,2,8,64,128]{4,3,2,1,0:T(8,128)(2,1)}, u32[]{:S(2)}, u32[]{:S(2)}) %collective-permute-start.12) | collective-permute-done | bytes 524320 | tf_op jit(solution)/shard_map/cond/branch_4_fun/ppermute | solution.py:354
  83.4 1.3 collective-permute-done.13
  84.7 6.6 %all-to-all-start.7 = ((bf16[8,4,4,64,128]{4,3,2,1,0:T(8,128)(2,1)}), bf16[8,4,4,64,128]{4,3,2,1,0:T(8,128)(2,1)}, u32[]{:S(2)}, u32[]{:S(2)}) async-start(bf16[8,4,4,64,128]{4,3,2,1,0:T(8,128)(2,1)} %temporal.9), calls=%async_computation.7 | async-start | bytes 4194304 | tf_op jit(solution)/shard_map/cond/branch_4_fun/all_to_all | solution.py:376
  91.3 0.0 copy-done.14
  91.3 7.7 %spatial.10 = (bf16[512,768]{1,0:T(8,128)(2,1)}, bf16[512,768]{1,0:T(8,128)(2,1)}, f32[2,2,512,128]{3,2,1,0:T(8,128)}, f32[2,2,512]{2,1,0:T(2,128)}) custom-call(s32[24]{0:T(128)S(1)} %copy-done.21, s32[1]{0:T(128)} %get-tuple-element.294.first_ref, s32[1]{0:T(128)} %get-tuple-element.306.frame_ref, bf16[512,768]{1,0:T(8,128)(2,1)S(1)} %bitcast.167, ...), custom_call_target="tpu_custom_call" | custom-call | flops 1342177280 | bytes 2097152 | tf_op jit(solution)/shard_map/cond/branch_4_fun/spatial/pallas_call | solution.py:295
  98.9 2.5 %collective-permute-start.14 = (f32[2,2,512]{2,1,0:T(2,128)}, f32[2,2,512]{2,1,0:T(2,128)S(1)}, u32[]{:S(2)}, u32[]{:S(2)}) collective-permute-start(f32[2,2,512]{2,1,0:T(2,128)} %get-tuple-element.315), channel_id=1, source_target_pairs={{4,0},{8,4},{12,8},{16,12},{20,16},{24,20},{28,24},{5,1},{9,5},{13... | collective-permute-start | bytes 24584 | tf_op jit(solution)/shard_map/cond/branch_4_fun/ppermute | solution.py:354
  101.4 41.1 %collective-permute-done.14.stats_ref = f32[2,2,512]{2,1,0:T(2,128)S(1)} collective-permute-done((f32[2,2,512]{2,1,0:T(2,128)}, f32[2,2,512]{2,1,0:T(2,128)S(1)}, u32[]{:S(2)}, u32[]{:S(2)}) %collective-permute-start.14) | collective-permute-done | bytes 8224 | tf_op jit(solution)/shard_map/cond/branch_4_fun/ppermute | solution.py:354
  142.5 0.0 copy-start.35
  142.5 0.6 copy-done.35
  143.0 4.4 %spatial_next.10 = (bf16[512,768]{1,0:T(8,128)(2,1)}, bf16[512,768]{1,0:T(8,128)(2,1)}) custom-call(s32[24]{0:T(128)S(1)} %copy-done.21, s32[1]{0:T(128)} %get-tuple-element.294.first_ref, bf16[512,768]{1,0:T(8,128)(2,1)S(1)} %bitcast.114, bf16[512,768]{1,0:T(8,128)(2,1)S(1)} %bitcast.143, bf16[2,2,512,128]{3,2,1,0:T(8,128)(2,1)} %bitcast.59.next_ref, ...), custom_call_target="tpu_custom_call" | custom-call | flops 536870912 | bytes 2621440 | tf_op jit(solution)/shard_map/cond/branch_4_fun/spatial_next/pallas_call | solution.py:335
  147.5 0.0 all-to-all-done.7.in_ref
  147.5 3.1 %unpack.9 = (bf16[8,64,768]{2,1,0:T(8,128)(2,1)}, bf16[8,64,768]{2,1,0:T(8,128)(2,1)}, bf16[8,64,768]{2,1,0:T(8,128)(2,1)}, bf16[8,64,768]{2,1,0:T(8,128)(2,1)}) custom-call(s32[24]{0:T(128)S(1)} %copy-done.21, s32[1]{0:T(128)} %get-tuple-element.294.first_ref, ...), custom_call_target="tpu_custom_call", output_to_operand_aliasing={{0}: (3, {}), {1}: (4, {}), {2}: (5, {}), {3}: (6, {})} | custom-call | bytes 4194304 | tf_op jit(solution)/shard_map/cond/branch_4_fun/unpack/pallas_call | solution.py:234
Async XLA Ops:
  6.2 6.4 %copy-start.4 = (bf16[1,512,768]{2,1,0:T(8,128)(2,1)S(1)}, bf16[1,512,768]{2,1,0:T(8,128)(2,1)}, u32[]{:S(2)}) copy-start(bf16[1,512,768]{2,1,0:T(8,128)(2,1)} %get-tuple-element.308) | copy-start | bytes 2359300 | tf_op jit(solution)/shard_map/cond
  6.3 6.4 %copy-start.10 = (bf16[1,512,768]{2,1,0:T(8,128)(2,1)S(1)}, bf16[1,512,768]{2,1,0:T(8,128)(2,1)}, u32[]{:S(2)}) copy-start(bf16[1,512,768]{2,1,0:T(8,128)(2,1)} %get-tuple-element.309) | copy-start | bytes 2359300 | tf_op jit(solution)/shard_map/cond
  6.3 6.4 %copy-start.21 = (s32[24]{0:T(128)S(1)}, s32[24]{0:T(128)}, u32[]{:S(2)}) copy-start(s32[24]{0:T(128)} %get-tuple-element.293.kind_ref) | copy-start | bytes 292 | tf_op jit(solution)/shard_map/cond
  6.3 54.5 %all-to-all-start.6 = ((bf16[8,4,4,64,128]{4,3,2,1,0:T(8,128)(2,1)}), bf16[8,4,4,64,128]{4,3,2,1,0:T(8,128)(2,1)}, u32[]{:S(2)}, u32[]{:S(2)}) async-start(bf16[8,4,4,64,128]{4,3,2,1,0:T(8,128)(2,1)} %pack_temporal.9), calls=%async_computation.6 | async-start | bytes 4194304 | tf_op jit(solution)/shard_map/cond/branch_4_fun/all_to_all | solution.py:366
  12.7 54.4 %copy-start.30 = (s32[24]{0:T(128)S(1)}, s32[24]{0:T(128)}, u32[]{:S(2)}) copy-start(s32[24]{0:T(128)} %get-tuple-element.295.band_ref) | copy-start | bytes 292 | tf_op jit(solution)/shard_map/cond
  60.8 22.6 %collective-permute-start.12 = (bf16[2,2,8,64,128]{4,3,2,1,0:T(8,128)(2,1)}, bf16[2,2,8,64,128]{4,3,2,1,0:T(8,128)(2,1)}, u32[]{:S(2)}, u32[]{:S(2)}) collective-permute-start(bf16[2,2,8,64,128]{4,3,2,1,0:T(8,128)(2,1)} %get-tuple-element.303), channel_id=1, source_target_pairs={{0,4},{4,8},{8,12},{12,16},{16,20},{20,24},{24,28},{1,5},{5,9},{9,... | collective-permute-start | bytes 1572872 | tf_op jit(solution)/shard_map/cond/branch_4_fun/ppermute | solution.py:354
  65.2 19.5 %collective-permute-start.13 = (bf16[2,2,8,64,128]{4,3,2,1,0:T(8,128)(2,1)}, bf16[2,2,8,64,128]{4,3,2,1,0:T(8,128)(2,1)}, u32[]{:S(2)}, u32[]{:S(2)}) collective-permute-start(bf16[2,2,8,64,128]{4,3,2,1,0:T(8,128)(2,1)} %get-tuple-element.304), channel_id=1, source_target_pairs={{4,0},{8,4},{12,8},{16,12},{20,16},{24,20},{28,24},{5,1},{9,5},{13... | collective-permute-start | bytes 1572872 | tf_op jit(solution)/shard_map/cond/branch_4_fun/ppermute | solution.py:354
  73.0 18.3 %copy-start.14 = (bf16[1,512,768]{2,1,0:T(8,128)(2,1)S(1)}, bf16[1,512,768]{2,1,0:T(8,128)(2,1)}, u32[]{:S(2)}) copy-start(bf16[1,512,768]{2,1,0:T(8,128)(2,1)} %get-tuple-element.307) | copy-start | bytes 2359300 | tf_op jit(solution)/shard_map/cond
  84.7 62.8 %all-to-all-start.7 = ((bf16[8,4,4,64,128]{4,3,2,1,0:T(8,128)(2,1)}), bf16[8,4,4,64,128]{4,3,2,1,0:T(8,128)(2,1)}, u32[]{:S(2)}, u32[]{:S(2)}) async-start(bf16[8,4,4,64,128]{4,3,2,1,0:T(8,128)(2,1)} %temporal.9), calls=%async_computation.7 | async-start | bytes 4194304 | tf_op jit(solution)/shard_map/cond/branch_4_fun/all_to_all | solution.py:376
  98.9 43.5 %collective-permute-start.14 = (f32[2,2,512]{2,1,0:T(2,128)}, f32[2,2,512]{2,1,0:T(2,128)S(1)}, u32[]{:S(2)}, u32[]{:S(2)}) collective-permute-start(f32[2,2,512]{2,1,0:T(2,128)} %get-tuple-element.315), channel_id=1, source_target_pairs={{4,0},{8,4},{12,8},{16,12},{20,16},{24,20},{28,24},{5,1},{9,5},{13... | collective-permute-start | bytes 24584 | tf_op jit(solution)/shard_map/cond/branch_4_fun/ppermute | solution.py:354
  142.5 0.6 copy-start.35

commit v3 on v2

--- a/solution.py
+++ b/solution.py
@@ -219,31 +219,25 @@
 
 def unpack(kinds, first, rows_in, filled, heads):
     frames, _, slots, rows, _ = rows_in.shape
+    count = frames * rows
+    held = len(filled)
 
     def kernel(kind_ref, first_ref, in_ref, *refs):
-        outs, (stage, in_sems, out_sems) = refs[-7:-3], refs[-3:]
-        triples = []
-        for slot in range(slots):
-            cols = head_columns(kind_ref, first_ref, heads, TEMPORAL, slot)
-            for place, ref in enumerate(outs):
-                triples.append(
-                    (in_ref.at[:, place, slot], stage.at[slot, place], ref.at[:, :, cols])
-                )
-        staged_copies(triples, in_sems, out_sems)
-
-    return pl.pallas_call(
-        kernel,
-        out_shape=[jax.ShapeDtypeStruct((frames, rows, heads * DH), BF16)] * 4,
-        in_specs=[pl.BlockSpec(memory_space=pltpu.SMEM)] * 2
-        + [pl.BlockSpec(memory_space=pl.ANY)] * (1 + len(filled)),
-        out_specs=[pl.BlockSpec(memory_space=pl.ANY)] * 4,
-        scratch_shapes=[
-            pltpu.VMEM((slots, 4, frames, rows, DH), BF16),
-            pltpu.SemaphoreType.DMA((4 * slots,)),
-            pltpu.SemaphoreType.DMA((4 * slots,)),
-        ],
-        input_output_aliases={3 + place: place for place in range(len(filled))},
-        compiler_params=whole_params(),
+        for place, ref in enumerate(refs[held:]):
+            ref[...] = in_ref[:, place, 0].reshape(count, DH)
+
+    block = pl.BlockSpec((frames, 4, 1, rows, DH), lambda i, *refs: (0, 0, i, 0, 0))
+    return pl.pallas_call(
+        kernel,
+        out_shape=[jax.ShapeDtypeStruct((count, heads * DH), BF16)] * 4,
+        grid_spec=pltpu.PrefetchScalarGridSpec(
+            num_scalar_prefetch=2,
+            grid=(slots,),
+            in_specs=[block] + [pl.BlockSpec(memory_space=pl.ANY)] * held,
+            out_specs=[column_spec(count, heads, TEMPORAL)] * 4,
+        ),
+        input_output_aliases={3 + place: place for place in range(held)},
+        compiler_params=params(),
         cost_estimate=cost(0, 4 * rows_in.size),
         name="unpack",
     )(kinds, first, rows_in, *filled)
@@ -261,9 +255,11 @@
         has_prior = frame_ref[0] > 0
         k, v = k_ref[...], v_ref[...]
         k_prior, v_prior = prior_ref[0, 0], prior_ref[0, 1]
-        k_own = v_own = None
-        for start in range(0, count, chunk):
-            part = slice(start, start + chunk)
+        own_ref[...] = jnp.zeros_like(own_ref)
+
+        @pl.loop(0, count // chunk)
+        def _(step):
+            part = pl.ds(pl.multiple_of(step * chunk, chunk), chunk)
             q, g = q_ref[part], g_ref[part]
             own = dot_nt(q, k) * SCALE
             before = jnp.where(has_prior, dot_nt(q, k_prior) * SCALE, MASKED)
@@ -281,13 +277,11 @@
             before_ds = (before * (dot_nt(g, v_prior) - delta) * SCALE).astype(BF16)
             out_ref[part] = attended
             qgrad_ref[part] = (dot_nn(own_ds, k) + dot_nn(before_ds, k_prior)).astype(BF16)
-            k_term, v_term = dot_tn(own_ds, q), dot_tn(own_prob, g)
-            k_own = k_term if start == 0 else k_own + k_term
-            v_own = v_term if start == 0 else v_own + v_term
+            own_ref[0, 0] += dot_tn(own_ds, q)
+            own_ref[0, 1] += dot_tn(own_prob, g)
             lane = lax.broadcasted_iota(jnp.int32, (chunk, DH), 1)
             stats = jnp.where(lane == 0, top + jnp.log(total), delta)
             stats_ref[0, :, part] = stats.T[:2]
-        own_ref[0, 0], own_ref[0, 1] = k_own, v_own
 
     columns = column_spec(count, heads, SPATIAL)
     pair = pl.BlockSpec((1, 2, count, DH), lambda i, *refs: (i, 0, 0, 0))
@@ -314,17 +308,23 @@
     )(kinds, first, frame, *arrays, prior)
 
 
-def spatial_next(kinds, first, k, v, following, stats, own, heads):
+def spatial_next(kinds, first, frame, k, v, following, stats, own, heads):
     slots, _, count, _ = own.shape
+    frames = stats.shape[0]
     chunk = min(count, 256)
 
     def kernel(
-        kind_ref, first_ref, k_ref, v_ref, next_ref, stats_ref, own_ref, kgrad_ref, vgrad_ref
+        kind_ref, first_ref, frame_ref, k_ref, v_ref, next_ref, stats_ref, own_ref,
+        kgrad_ref, vgrad_ref,
     ):
         q, g = next_ref[0, 0], next_ref[0, 1]
-        lse, delta = stats_ref[0, 0:1], stats_ref[0, 1:2]
-        for start in range(0, count, chunk):
-            part = slice(start, start + chunk)
+        has_next = frame_ref[0] < frames - 1
+        lse = jnp.where(has_next, stats_ref[0, 0, 0:1], 0.0)
+        delta = jnp.where(has_next, stats_ref[0, 0, 1:2], 0.0)
+
+        @pl.loop(0, count // chunk)
+        def _(step):
+            part = pl.ds(pl.multiple_of(step * chunk, chunk), chunk)
             weight = jnp.exp(dot_nt(k_ref[part], q) * SCALE - lse)
             dscore = (weight * (dot_nt(v_ref[part], g) - delta) * SCALE).astype(BF16)
             kgrad_ref[part] = (own_ref[0, 0, part] + dot_nn(dscore, q)).astype(BF16)
@@ -332,26 +332,32 @@
 
     columns = column_spec(count, heads, SPATIAL)
     pair = pl.BlockSpec((1, 2, count, DH), lambda i, *refs: (i, 0, 0, 0))
+    after = pl.BlockSpec(
+        (1, 1, 2, count), lambda i, *refs: (jnp.minimum(refs[2][0] + 1, frames - 1), i, 0, 0)
+    )
     return pl.pallas_call(
         kernel,
         out_shape=[jax.ShapeDtypeStruct((count, heads * DH), BF16)] * 2,
         grid_spec=pltpu.PrefetchScalarGridSpec(
-            num_scalar_prefetch=2,
+            num_scalar_prefetch=3,
             grid=(slots,),
-            in_specs=[columns, columns, pair]
-            + [pl.BlockSpec((1, 2, count), lambda i, *refs: (i, 0, 0)), pair],
+            in_specs=[columns, columns, pair, after, pair],
             out_specs=[columns] * 2,
         ),
-        compiler_params=params(60),
+        compiler_params=params(),
         cost_estimate=cost(8 * slots * count * count * DH, 20 * slots * count * DH),
         name="spatial_next",
-    )(kinds, first, k, v, following, stats, own)
+    )(kinds, first, frame, k, v, following, stats, own)
 
 
 def passed_along(array, axis, by):
     length = lax.axis_size(axis)
     pairs = [(i, i + by) for i in range(length) if 0 <= i + by < length]
     return lax.ppermute(array, axis, pairs)
+
+
+def behind(arrays, *others):
+    return lax.optimization_barrier((tuple(arrays), others))[0]
 
 
 def branch(slots, heads, kinds, bands, first, frame, q, k, v, g):
@@ -364,23 +370,19 @@
     filled = ()
     if slots > 0:
         framed = exchange(pack_temporal(kinds, first, (q, k, v, g), slots, heads))
+        results = temporal(kinds, first, bands, framed, heads)
+        returned = exchange(results)
     if others > 0:
         ahead, back = pack_spatial(kinds, first, (k, v, q, g), others, heads)
+        arrived = [passed_along(ahead, "ctx", 1), passed_along(back, "ctx", -1)]
         if slots > 0:
-            framed, ahead, back = lax.optimization_barrier((framed, ahead, back))
-        prior, following = passed_along(ahead, "ctx", 1), passed_along(back, "ctx", -1)
-    if slots > 0:
-        results = temporal(kinds, first, bands, framed, heads)
-        if others > 0:
-            results, prior, following = lax.optimization_barrier((results, prior, following))
-        returned = exchange(results)
-    if others > 0:
-        prior, following = (x.reshape(others, 2, count, DH) for x in (prior, following))
+            arrived = behind(arrived, results)
+        prior, following = (x.reshape(others, 2, count, DH) for x in arrived)
         flat = [x.reshape(count, width) for x in (q, k, v, g)]
         attended, qgrad, own, stats = spatial(kinds, first, frame, flat, prior, heads)
-        stats = passed_along(stats, "ctx", -1)
-        grads = spatial_next(kinds, first, flat[1], flat[2], following, stats, own, heads)
-        filled = tuple(x.reshape(q.shape) for x in (attended, qgrad, *grads))
+        stats = lax.all_gather(stats, "ctx")
+        grads = spatial_next(kinds, first, frame, flat[1], flat[2], following, stats, own, heads)
+        filled = (attended, qgrad, *grads)
     if slots > 0:
         filled = unpack(kinds, first, returned, filled, heads)
     return tuple(filled)

time: 150 us -> 179 us (1.19)
  the two profiles are of different devices: /device:TPU:14 before, /device:TPU:2 now
where the time goes in v3:
time: 179 us; the launch traced here: 177 us
  blocking collectives  112 us (63%)
  Pallas kernels  25.6 us (14%)
  waiting for transfers between devices  24.3 us (14%)
  starting transfers between devices  9.64 us (5%)
  local copies, waits for them, and re-layouts  2.64 us (1%)
    all_to_all x1, blocking collectives, branch(): framed = exchange(pack_temporal(kinds, first, (q, k, v, g), slots, heads))  59.6 us
    all_gather x1, blocking collectives, branch(): stats = lax.all_gather(stats, 'ctx')  52.7 us
    ppermute x2, waiting for transfers between devices, passed_along(): return lax.ppermute(array, axis, pairs)  24.3 us
    pallas_call x1, Pallas kernels, temporal(): pl.pallas_call(kernel, out_shape=jax.ShapeDtypeStruct(rows_in.shape, BF16...  6.74 us
    pallas_call x1, Pallas kernels, unpack(): pl.pallas_call(kernel, out_shape=[jax.ShapeDtypeStruct((count, heads * DH...  5.34 us
    pallas_call x1, Pallas kernels, spatial(): pl.pallas_call(kernel, out_shape=[whole, whole, jax.ShapeDtypeStruct(prio...  5.15 us
    ppermute x2, starting transfers between devices, passed_along(): return lax.ppermute(array, axis, pairs)  5.09 us
    all_to_all x1, starting transfers between devices, branch(): returned = exchange(results)  4.54 us
  transfers between devices with their start and end apart: 3, of which 1 were waited for; matrix products, arithmetic and copies ran while one was open for 0% of the time, Pallas kernels for 6%

profile of v3, /device:TPU:2, one launch (start us, length us, event | category | flops | bytes accessed | tf_op | source)
XLA Modules:
  0.0 177.5 jit_solution(9960028452950431631)
XLA Ops:
  0.6 1.4 fusion
  2.7 174.8 %conditional.1 = ((bf16[512,768]{1,0:T(8,128)(2,1)}, bf16[512,768]{1,0:T(8,128)(2,1)}, bf16[512,768]{1,0:T(8,128)(2,1)}, bf16[512,768]{1,0:T(8,128)(2,1)})) conditional(s32[]{:T(128)} %clamp.3, (bf16[1,512,768]{2,1,0:T(8,128)(2,1)}, bf16[1,512,768]{2,1,0:T(8,128)(2,1)}, bf16[1,512,768]{2,1,0:T(8,128)(2,1)}, ...), branch_computations={%region_1.0_spmd, %region_2.0_spmd, %region_3.0_spmd, %region_4.0_... | conditional | flops 5637144576 | bytes 53924928 | solution.py:403
  2.9 3.6 %pack_temporal.10 = bf16[8,4,5,64,128]{4,3,2,1,0:T(8,128)(2,1)} custom-call(s32[24]{0:T(128)} %get-tuple-element.263.kind_ref, s32[1]{0:T(128)} %get-tuple-element.264.first_ref, bf16[8,64,768]{2,1,0:T(8,128)(2,1)} %bitcast.142, bf16[8,64,768]{2,1,0:T(8,128)(2,1)} %bitcast.89, bf16[8,64,768]{2,1,0:T(8,128)(2,1)} %bitcast.118, bf16[8,64,768]{2,1,0:T(8,128)(2,1)} %bitcast.165), custom_call_target="tpu_custom_call" | custom-call | bytes 5242880 | tf_op jit(solution)/shard_map/cond/branch_5_fun/pack_temporal/pallas_call | solution.py:123
  6.5 0.0 copy-start.24
  6.5 0.0 copy-start.31
  6.5 59.6 %all_to_all.51.rows_ref = bf16[8,4,5,64,128]{4,3,2,1,0:T(8,128)(2,1)} all-to-all(bf16[8,4,5,64,128]{4,3,2,1,0:T(8,128)(2,1)} %pack_temporal.10), channel_id=1, replica_groups=mesh['ctx'=8,'head'=4] {'ctx'}, dimensions={0} | all-to-all | bytes 5242880 | tf_op jit(solution)/shard_map/cond/branch_5_fun/all_to_all | solution.py:372
  66.2 0.0 copy-done.24
  66.2 0.0 copy-done.31
  66.2 6.7 %temporal.10 = bf16[8,4,5,64,128]{4,3,2,1,0:T(8,128)(2,1)} custom-call(s32[24]{0:T(128)S(1)} %copy-done.24, s32[1]{0:T(128)} %get-tuple-element.264.first_ref, s32[24]{0:T(128)S(1)} %copy-done.31, bf16[8,4,5,64,128]{4,3,2,1,0:T(8,128)(2,1)} %all_to_all.51.rows_ref), custom_call_target="tpu_custom_call" | custom-call | flops 503316480 | bytes 5242880 | tf_op jit(solution)/shard_map/cond/branch_5_fun/temporal/pallas_call | solution.py:202
  72.9 0.0 copy-start.12
  72.9 0.0 copy-start.17
  72.9 4.5 %all-to-all-start.9 = ((bf16[8,4,5,64,128]{4,3,2,1,0:T(8,128)(2,1)}), bf16[8,4,5,64,128]{4,3,2,1,0:T(8,128)(2,1)}, u32[]{:S(2)}, u32[]{:S(2)}) async-start(bf16[8,4,5,64,128]{4,3,2,1,0:T(8,128)(2,1)} %temporal.10), calls=%async_computation.9 | async-start | bytes 5242880 | tf_op jit(solution)/shard_map/cond/branch_5_fun/all_to_all | solution.py:374
  77.5 0.0 copy-done.12
  77.5 0.0 copy-done.17
  77.5 2.4 %pack_spatial.11 = (bf16[1,2,8,64,128]{4,3,2,1,0:T(8,128)(2,1)}, bf16[1,2,8,64,128]{4,3,2,1,0:T(8,128)(2,1)}) custom-call(s32[24]{0:T(128)S(1)} %copy-done.24, s32[1]{0:T(128)} %get-tuple-element.264.first_ref, bf16[8,64,768]{2,1,0:T(8,128)(2,1)S(1)} %bitcast.90, bf16[8,64,768]{2,1,0:T(8,128)(2,1)S(1)} %bitcast.119, bf16[8,64,768]{2,1,0:T(8,128)(2,1)} %bitcast.143, ...), custom_call_target="tpu_custom_call" | custom-call | bytes 1048576 | tf_op jit(solution)/shard_map/cond/branch_5_fun/pack_spatial/pallas_call | solution.py:91
  79.9 3.8 %collective-permute-start.10 = (bf16[1,2,8,64,128]{4,3,2,1,0:T(8,128)(2,1)}, bf16[1,2,8,64,128]{4,3,2,1,0:T(8,128)(2,1)S(1)}, u32[]{:S(2)}, u32[]{:S(2)}) collective-permute-start(bf16[1,2,8,64,128]{4,3,2,1,0:T(8,128)(2,1)} %get-tuple-element.275), channel_id=1, source_target_pairs={{0,4},{4,8},{8,12},{12,16},{16,20},{20,24},{24,28},{1,5},{5,9},{9,... | collective-permute-start | bytes 786440 | tf_op jit(solution)/shard_map/cond/branch_5_fun/ppermute | solution.py:356
  83.7 1.3 collective-permute-start.11
  85.0 24.3 %collective-permute-done.10 = bf16[1,2,8,64,128]{4,3,2,1,0:T(8,128)(2,1)S(1)} collective-permute-done((bf16[1,2,8,64,128]{4,3,2,1,0:T(8,128)(2,1)}, bf16[1,2,8,64,128]{4,3,2,1,0:T(8,128)(2,1)S(1)}, u32[]{:S(2)}, u32[]{:S(2)}) %collective-permute-start.10) | collective-permute-done | bytes 262176 | tf_op jit(solution)/shard_map/cond/branch_5_fun/ppermute | solution.py:356
  109.3 0.0 copy-start.26
  109.3 0.0 collective-permute-done.11
  109.3 0.7 copy-done.26
  110.0 5.2 %spatial.11 = (bf16[512,768]{1,0:T(8,128)(2,1)S(1)}, bf16[512,768]{1,0:T(8,128)(2,1)}, f32[1,2,512,128]{3,2,1,0:T(8,128)}, f32[1,2,512]{2,1,0:T(2,128)}) custom-call(s32[24]{0:T(128)S(1)} %copy-done.24, s32[1]{0:T(128)} %get-tuple-element.264.first_ref, s32[1]{0:T(128)} %get-tuple-element.270.frame_ref, bf16[512,768]{1,0:T(8,128)(2,1)} %bitcast.144, ...), custom_call_target="tpu_custom_call" | custom-call | flops 671088640 | bytes 1048576 | tf_op jit(solution)/shard_map/cond/branch_5_fun/spatial/pallas_call | solution.py:289
  115.1 52.7 %all-gather.5 = f32[8,2,512]{2,1,0:T(2,128)S(1)} all-gather(f32[1,2,512]{2,1,0:T(2,128)} %get-tuple-element.281), channel_id=7, replica_groups=mesh['ctx'=8,'head'=4] {'ctx'}, dimensions={0}, use_global_device_ids=true | all-gather | bytes 36864 | tf_op jit(solution)/shard_map/cond/branch_5_fun/all_gather | solution.py:383
  167.8 0.0 copy-start.5
  167.8 1.0 copy-done.5
  168.9 2.4 %spatial_next.11 = (bf16[512,768]{1,0:T(8,128)(2,1)}, bf16[512,768]{1,0:T(8,128)(2,1)}) custom-call(s32[24]{0:T(128)S(1)} %copy-done.24, s32[1]{0:T(128)} %get-tuple-element.264.first_ref, s32[1]{0:T(128)} %get-tuple-element.270.frame_ref, bf16[512,768]{1,0:T(8,128)(2,1)S(1)} %bitcast.92, bf16[512,768]{1,0:T(8,128)(2,1)S(1)} %bitcast.121, ...), custom_call_target="tpu_custom_call" | custom-call | flops 268435456 | bytes 1310720 | tf_op jit(solution)/shard_map/cond/branch_5_fun/spatial_next/pallas_call | solution.py:338
  171.2 0.0 all-to-all-done.9.in_ref
  171.2 5.3 %unpack.10 = (bf16[512,768]{1,0:T(8,128)(2,1)S(1)}, bf16[512,768]{1,0:T(8,128)(2,1)}, bf16[512,768]{1,0:T(8,128)(2,1)}, bf16[512,768]{1,0:T(8,128)(2,1)}) custom-call(s32[24]{0:T(128)S(1)} %copy-done.24, s32[1]{0:T(128)} %get-tuple-element.264.first_ref, ...), custom_call_target="tpu_custom_call", output_to_operand_aliasing={{0}: (3, {}), {1}: (4, {}), {2}: (5, {}), {3}: (6, {})} | custom-call | bytes 5242880 | tf_op jit(solution)/shard_map/cond/branch_5_fun/unpack/pallas_call | solution.py:230
  176.6 0.0 copy-start.18
  176.6 0.9 copy-done.18
Async XLA Ops:
  6.5 59.7 %copy-start.24 = (s32[24]{0:T(128)S(1)}, s32[24]{0:T(128)}, u32[]{:S(2)}) copy-start(s32[24]{0:T(128)} %get-tuple-element.263.kind_ref) | copy-start | bytes 292 | tf_op jit(solution)/shard_map/cond
  6.5 59.6 %copy-start.31 = (s32[24]{0:T(128)S(1)}, s32[24]{0:T(128)}, u32[]{:S(2)}) copy-start(s32[24]{0:T(128)} %get-tuple-element.265.band_ref) | copy-start | bytes 292 | tf_op jit(solution)/shard_map/cond
  72.9 4.6 %copy-start.12 = (bf16[1,512,768]{2,1,0:T(8,128)(2,1)S(1)}, bf16[1,512,768]{2,1,0:T(8,128)(2,1)}, u32[]{:S(2)}) copy-start(bf16[1,512,768]{2,1,0:T(8,128)(2,1)} %get-tuple-element.272) | copy-start | bytes 2359300 | tf_op jit(solution)/shard_map/cond
  72.9 4.6 %copy-start.17 = (bf16[1,512,768]{2,1,0:T(8,128)(2,1)S(1)}, bf16[1,512,768]{2,1,0:T(8,128)(2,1)}, u32[]{:S(2)}) copy-start(bf16[1,512,768]{2,1,0:T(8,128)(2,1)} %get-tuple-element.273) | copy-start | bytes 2359300 | tf_op jit(solution)/shard_map/cond
  72.9 98.3 %all-to-all-start.9 = ((bf16[8,4,5,64,128]{4,3,2,1,0:T(8,128)(2,1)}), bf16[8,4,5,64,128]{4,3,2,1,0:T(8,128)(2,1)}, u32[]{:S(2)}, u32[]{:S(2)}) async-start(bf16[8,4,5,64,128]{4,3,2,1,0:T(8,128)(2,1)} %temporal.10), calls=%async_computation.9 | async-start | bytes 5242880 | tf_op jit(solution)/shard_map/cond/branch_5_fun/all_to_all | solution.py:374
  79.9 29.4 %collective-permute-start.10 = (bf16[1,2,8,64,128]{4,3,2,1,0:T(8,128)(2,1)}, bf16[1,2,8,64,128]{4,3,2,1,0:T(8,128)(2,1)S(1)}, u32[]{:S(2)}, u32[]{:S(2)}) collective-permute-start(bf16[1,2,8,64,128]{4,3,2,1,0:T(8,128)(2,1)} %get-tuple-element.275), channel_id=1, source_target_pairs={{0,4},{4,8},{8,12},{12,16},{16,20},{20,24},{24,28},{1,5},{5,9},{9,... | collective-permute-start | bytes 786440 | tf_op jit(solution)/shard_map/cond/branch_5_fun/ppermute | solution.py:356
  83.7 25.6 %collective-permute-start.11 = (bf16[1,2,8,64,128]{4,3,2,1,0:T(8,128)(2,1)}, bf16[1,2,8,64,128]{4,3,2,1,0:T(8,128)(2,1)S(1)}, u32[]{:S(2)}, u32[]{:S(2)}) collective-permute-start(bf16[1,2,8,64,128]{4,3,2,1,0:T(8,128)(2,1)} %get-tuple-element.276), channel_id=1, source_target_pairs={{4,0},{8,4},{12,8},{16,12},{20,16},{24,20},{28,24},{5,1},{9,5},{13... | collective-permute-start | bytes 786440 | tf_op jit(solution)/shard_map/cond/branch_5_fun/ppermute | solution.py:356
  109.3 0.7 copy-start.26
  167.8 1.0 copy-start.5
  176.6 0.9 copy-start.18

commit v4 on v3

--- a/solution.py
+++ b/solution.py
@@ -37,9 +37,9 @@
     return lax.dot_general(a, b, (((0,), (0,)), ((), ())), preferred_element_type=F32)
 
 
-def params(mib=32):
+def params(mib=32, grid=True):
     return pltpu.CompilerParams(
-        dimension_semantics=("arbitrary",), vmem_limit_bytes=mib * MIB
+        dimension_semantics=("arbitrary",) if grid else None, vmem_limit_bytes=mib * MIB
     )
 
 
@@ -71,29 +71,27 @@
     return pltpu.CompilerParams(vmem_limit_bytes=62 * MIB)
 
 
-def pack_spatial(kinds, first, arrays, slots, heads):
+def pack_spatial(kinds, first, arrays, slots, heads, after):
     frames, rows, _ = arrays[0].shape
     count = len(arrays)
     total = slots * count
 
     def kernel(kind_ref, first_ref, *refs):
-        ins, outs = refs[:count], refs[count:-3]
+        ins, outs = refs[:count], refs[-3 - count : -3]
         stage, in_sems, out_sems = refs[-3:]
         triples = []
         for slot in range(slots):
             cols = head_columns(kind_ref, first_ref, heads, SPATIAL, slot)
-            for place, ref in enumerate(ins):
-                target = outs[place // 2].at[slot, place % 2]
-                triples.append((ref.at[:, :, cols], stage.at[slot, place], target))
+            for place, (ref, out) in enumerate(zip(ins, outs)):
+                triples.append((ref.at[:, :, cols], stage.at[slot, place], out.at[slot]))
         staged_copies(triples, in_sems, out_sems)
 
-    pair = jax.ShapeDtypeStruct((slots, 2, frames, rows, DH), BF16)
     return pl.pallas_call(
         kernel,
-        out_shape=[pair] * (count // 2),
+        out_shape=[jax.ShapeDtypeStruct((slots, frames, rows, DH), BF16)] * count,
         in_specs=[pl.BlockSpec(memory_space=pltpu.SMEM)] * 2
-        + [pl.BlockSpec(memory_space=pl.ANY)] * count,
-        out_specs=[pl.BlockSpec(memory_space=pl.ANY)] * (count // 2),
+        + [pl.BlockSpec(memory_space=pl.ANY)] * (count + len(after)),
+        out_specs=[pl.BlockSpec(memory_space=pl.ANY)] * count,
         scratch_shapes=[
             pltpu.VMEM((slots, count, frames, rows, DH), BF16),
             pltpu.SemaphoreType.DMA((total,)),
@@ -102,7 +100,7 @@
         compiler_params=whole_params(),
         cost_estimate=cost(0, 4 * total * frames * rows * DH),
         name="pack_spatial",
-    )(kinds, first, *arrays)
+    )(kinds, first, *arrays, *after)
 
 
 def pack_temporal(kinds, first, arrays, slots, heads):
@@ -212,49 +210,23 @@
             pltpu.SemaphoreType.DMA((slots,)),
         ],
         compiler_params=whole_params(),
-        cost_estimate=cost(12 * slots * rows * frames * size * DH, 4 * rows_in.size),
+        cost_estimate=cost(1e10, 4 * rows_in.size),
         name="temporal",
     )(kinds, first, bands, rows_in)
 
 
-def unpack(kinds, first, rows_in, filled, heads):
-    frames, _, slots, rows, _ = rows_in.shape
-    count = frames * rows
-    held = len(filled)
-
-    def kernel(kind_ref, first_ref, in_ref, *refs):
-        for place, ref in enumerate(refs[held:]):
-            ref[...] = in_ref[:, place, 0].reshape(count, DH)
-
-    block = pl.BlockSpec((frames, 4, 1, rows, DH), lambda i, *refs: (0, 0, i, 0, 0))
-    return pl.pallas_call(
-        kernel,
-        out_shape=[jax.ShapeDtypeStruct((count, heads * DH), BF16)] * 4,
-        grid_spec=pltpu.PrefetchScalarGridSpec(
-            num_scalar_prefetch=2,
-            grid=(slots,),
-            in_specs=[block] + [pl.BlockSpec(memory_space=pl.ANY)] * held,
-            out_specs=[column_spec(count, heads, TEMPORAL)] * 4,
-        ),
-        input_output_aliases={3 + place: place for place in range(held)},
-        compiler_params=params(),
-        cost_estimate=cost(0, 4 * rows_in.size),
-        name="unpack",
-    )(kinds, first, rows_in, *filled)
-
-
-def spatial(kinds, first, frame, arrays, prior, heads):
+def spatial(kinds, first, frame, arrays, k_prior, v_prior, heads):
     count = arrays[0].shape[0]
-    slots = prior.shape[0]
+    slots = k_prior.shape[0]
     chunk = min(count, 256)
 
     def kernel(
-        kind_ref, first_ref, frame_ref, q_ref, k_ref, v_ref, g_ref, prior_ref,
+        kind_ref, first_ref, frame_ref, q_ref, k_ref, v_ref, g_ref, k_prior_ref, v_prior_ref,
         out_ref, qgrad_ref, own_ref, stats_ref,
     ):
         has_prior = frame_ref[0] > 0
         k, v = k_ref[...], v_ref[...]
-        k_prior, v_prior = prior_ref[0, 0], prior_ref[0, 1]
+        k_prior, v_prior = k_prior_ref[0], v_prior_ref[0]
         own_ref[...] = jnp.zeros_like(own_ref)
 
         @pl.loop(0, count // chunk)
@@ -284,6 +256,7 @@
             stats_ref[0, :, part] = stats.T[:2]
 
     columns = column_spec(count, heads, SPATIAL)
+    single = pl.BlockSpec((1, count, DH), lambda i, *refs: (i, 0, 0))
     pair = pl.BlockSpec((1, 2, count, DH), lambda i, *refs: (i, 0, 0, 0))
     whole = jax.ShapeDtypeStruct((count, heads * DH), BF16)
     return pl.pallas_call(
@@ -291,63 +264,124 @@
         out_shape=[
             whole,
             whole,
-            jax.ShapeDtypeStruct(prior.shape, F32),
+            jax.ShapeDtypeStruct((slots, 2, count, DH), F32),
             jax.ShapeDtypeStruct((slots, 2, count), F32),
         ],
         grid_spec=pltpu.PrefetchScalarGridSpec(
             num_scalar_prefetch=3,
             grid=(slots,),
-            in_specs=[columns] * 4 + [pair],
+            in_specs=[columns] * 4 + [single] * 2,
             out_specs=[
                 columns, columns, pair, pl.BlockSpec((1, 2, count), lambda i, *refs: (i, 0, 0))
             ],
         ),
         compiler_params=params(60),
-        cost_estimate=cost(20 * slots * count * count * DH, 16 * slots * count * DH),
+        cost_estimate=cost(2e11, 16 * slots * count * DH),
         name="spatial",
-    )(kinds, first, frame, *arrays, prior)
-
-
-def spatial_next(kinds, first, frame, k, v, following, stats, own, heads):
-    slots, _, count, _ = own.shape
-    frames = stats.shape[0]
+    )(kinds, first, frame, *arrays, k_prior, v_prior)
+
+
+def finish(kinds, first, frame, rows_in, filled, k, v, following, stats, own, heads):
+    count = k.shape[0]
+    slots = 0 if rows_in is None else rows_in.shape[2]
+    others = heads - slots
     chunk = min(count, 256)
-
-    def kernel(
-        kind_ref, first_ref, frame_ref, k_ref, v_ref, next_ref, stats_ref, own_ref,
-        kgrad_ref, vgrad_ref,
-    ):
-        q, g = next_ref[0, 0], next_ref[0, 1]
-        has_next = frame_ref[0] < frames - 1
-        lse = jnp.where(has_next, stats_ref[0, 0, 0:1], 0.0)
-        delta = jnp.where(has_next, stats_ref[0, 0, 1:2], 0.0)
-
-        @pl.loop(0, count // chunk)
-        def _(step):
-            part = pl.ds(pl.multiple_of(step * chunk, chunk), chunk)
-            weight = jnp.exp(dot_nt(k_ref[part], q) * SCALE - lse)
-            dscore = (weight * (dot_nt(v_ref[part], g) - delta) * SCALE).astype(BF16)
-            kgrad_ref[part] = (own_ref[0, 0, part] + dot_nn(dscore, q)).astype(BF16)
-            vgrad_ref[part] = (own_ref[0, 1, part] + dot_nn(weight.astype(BF16), g)).astype(BF16)
-
-    columns = column_spec(count, heads, SPATIAL)
-    pair = pl.BlockSpec((1, 2, count, DH), lambda i, *refs: (i, 0, 0, 0))
-    after = pl.BlockSpec(
-        (1, 1, 2, count), lambda i, *refs: (jnp.minimum(refs[2][0] + 1, frames - 1), i, 0, 0)
-    )
+    ins = ([] if rows_in is None else [rows_in]) + ([*filled, k, v, *following, stats, own] if others else [])
+    scratch = []
+    if slots:
+        frames, _, _, rows, _ = rows_in.shape
+        scratch += [pltpu.VMEM((slots, 4, frames, rows, DH), BF16)]
+        scratch += [pltpu.SemaphoreType.DMA((4 * slots,))] * 2
+    if others:
+        scratch += [pltpu.VMEM((others, 4, count, DH), BF16), pltpu.VMEM((others, 2, count, DH), F32)]
+        scratch += [pltpu.VMEM((others, 2, count), F32), pltpu.VMEM((others, 2, count, DH), BF16)]
+        scratch += [pltpu.SemaphoreType.DMA((8 * others,))]
+
+    def kernel(kind_ref, first_ref, *refs):
+        refs = list(refs)
+        in_refs, out_refs, temps = refs[: len(ins)], refs[len(ins) : len(ins) + 4], refs[len(ins) + 4 :]
+        loads, stores, next_loads, next_stores = [], [], [], []
+        if slots:
+            stage, in_sems, out_sems = temps[:3]
+            for slot in range(slots):
+                cols = head_columns(kind_ref, first_ref, heads, TEMPORAL, slot)
+                for place, out in enumerate(out_refs):
+                    at = 4 * slot + place
+                    held = stage.at[slot, place]
+                    loads.append(
+                        pltpu.make_async_copy(in_refs[0].at[:, place, slot], held, in_sems.at[at])
+                    )
+                    stores.append(
+                        pltpu.make_async_copy(
+                            held.reshape(count, DH), out.at[:, cols], out_sems.at[at]
+                        )
+                    )
+        if others:
+            rows_ref, own_ref, stats_ref, made_ref, sems = temps[-5:]
+            k_in, v_in, q_in, g_in, stats_in, own_in = in_refs[-6:]
+            for slot in range(others):
+                cols = head_columns(kind_ref, first_ref, heads, SPATIAL, slot)
+                pairs = [
+                    (k_in.at[:, cols], rows_ref.at[slot, 0]),
+                    (v_in.at[:, cols], rows_ref.at[slot, 1]),
+                    (q_in.at[slot], rows_ref.at[slot, 2]),
+                    (g_in.at[slot], rows_ref.at[slot, 3]),
+                    (stats_in.at[slot], stats_ref.at[slot]),
+                    (own_in.at[slot], own_ref.at[slot]),
+                ]
+                next_loads += [
+                    pltpu.make_async_copy(x, y, sems.at[8 * slot + i])
+                    for i, (x, y) in enumerate(pairs)
+                ]
+                next_stores += [
+                    pltpu.make_async_copy(
+                        made_ref.at[slot, i], out_refs[2 + i].at[:, cols], sems.at[8 * slot + 6 + i]
+                    )
+                    for i in range(2)
+                ]
+        for copy in next_loads + loads:
+            copy.start()
+        for load, store in zip(loads, stores):
+            load.wait()
+            store.start()
+        for copy in next_loads:
+            copy.wait()
+        if others:
+
+            @pl.loop(0, others)
+            def _(slot):
+                q, g = rows_ref[slot, 2], rows_ref[slot, 3]
+                lse, delta = stats_ref[slot, 0:1], stats_ref[slot, 1:2]
+
+                @pl.loop(0, count // chunk)
+                def _(step):
+                    part = pl.ds(pl.multiple_of(step * chunk, chunk), chunk)
+                    weight = jnp.exp(dot_nt(rows_ref[slot, 0, part], q) * SCALE - lse)
+                    dprob = dot_nt(rows_ref[slot, 1, part], g)
+                    dscore = (weight * (dprob - delta) * SCALE).astype(BF16)
+                    made_ref[slot, 0, part] = (own_ref[slot, 0, part] + dot_nn(dscore, q)).astype(BF16)
+                    made_ref[slot, 1, part] = (
+                        own_ref[slot, 1, part] + dot_nn(weight.astype(BF16), g)
+                    ).astype(BF16)
+
+        for copy in next_stores:
+            copy.start()
+        for copy in stores + next_stores:
+            copy.wait()
+
+    place = 2 + (1 if slots else 0)
     return pl.pallas_call(
         kernel,
-        out_shape=[jax.ShapeDtypeStruct((count, heads * DH), BF16)] * 2,
-        grid_spec=pltpu.PrefetchScalarGridSpec(
-            num_scalar_prefetch=3,
-            grid=(slots,),
-            in_specs=[columns, columns, pair, after, pair],
-            out_specs=[columns] * 2,
-        ),
-        compiler_params=params(),
-        cost_estimate=cost(8 * slots * count * count * DH, 20 * slots * count * DH),
-        name="spatial_next",
-    )(kinds, first, frame, k, v, following, stats, own)
+        out_shape=[jax.ShapeDtypeStruct((count, heads * DH), BF16)] * 4,
+        in_specs=[pl.BlockSpec(memory_space=pltpu.SMEM)] * 2
+        + [pl.BlockSpec(memory_space=pl.ANY)] * len(ins),
+        out_specs=[pl.BlockSpec(memory_space=pl.ANY)] * 4,
+        scratch_shapes=scratch,
+        input_output_aliases={place: 0, place + 1: 1} if others else {},
+        compiler_params=params(32, grid=False),
+        cost_estimate=cost(8 * others * count * count * DH, 16 * heads * count * DH),
+        name="finish",
+    )(kinds, first, *ins)
 
 
 def passed_along(array, axis, by):
@@ -367,25 +401,25 @@
     exchange = functools.partial(
         lax.all_to_all, axis_name="ctx", split_axis=0, concat_axis=0, tiled=True
     )
-    filled = ()
+    flat = [x.reshape(count, width) for x in (q, k, v, g)]
+    returned = filled = following = stats = own = None
+    packed = []
     if slots > 0:
-        framed = exchange(pack_temporal(kinds, first, (q, k, v, g), slots, heads))
+        packed = [pack_temporal(kinds, first, (q, k, v, g), slots, heads)]
+        framed = exchange(*packed)
         results = temporal(kinds, first, bands, framed, heads)
         returned = exchange(results)
     if others > 0:
-        ahead, back = pack_spatial(kinds, first, (k, v, q, g), others, heads)
-        arrived = [passed_along(ahead, "ctx", 1), passed_along(back, "ctx", -1)]
+        sent = pack_spatial(kinds, first, (k, v, q, g), others, heads, packed)
+        arrived = [passed_along(x, "ctx", by) for x, by in zip(sent, (1, 1, -1, -1))]
         if slots > 0:
             arrived = behind(arrived, results)
-        prior, following = (x.reshape(others, 2, count, DH) for x in arrived)
-        flat = [x.reshape(count, width) for x in (q, k, v, g)]
-        attended, qgrad, own, stats = spatial(kinds, first, frame, flat, prior, heads)
-        stats = lax.all_gather(stats, "ctx")
-        grads = spatial_next(kinds, first, frame, flat[1], flat[2], following, stats, own, heads)
-        filled = (attended, qgrad, *grads)
-    if slots > 0:
-        filled = unpack(kinds, first, returned, filled, heads)
-    return tuple(filled)
+        arrived = [x.reshape(others, count, DH) for x in arrived]
+        *filled, own, stats = spatial(kinds, first, frame, flat, *arrived[:2], heads)
+        following, stats = arrived[2:], passed_along(stats, "ctx", -1)
+    return finish(
+        kinds, first, frame, returned, filled, *flat[1:3], following, stats, own, heads
+    )
 
 
 def body(queries, key_rows, value_rows, out_grad, head_kind, frame_band):

time: 179 us -> 134 us (0.75)
  the two profiles are of different devices: /device:TPU:2 before, /device:TPU:14 now
where the time goes in v4:
time: 134 us; the launch traced here: 133 us
  waiting for transfers between devices  74.2 us (55%)
  starting transfers between devices  30.8 us (23%)
  Pallas kernels  22.9 us (17%)
  local copies, waits for them, and re-layouts  1.7 us (1%)
  between operations  1.47 us (1%)
  other arithmetic  1.37 us (1%)
    all_to_all x1, waiting for transfers between devices, branch(): framed = exchange(*packed)  38.2 us
    ppermute x5, waiting for transfers between devices, passed_along(): return lax.ppermute(array, axis, pairs)  36 us
    ppermute x5, starting transfers between devices, passed_along(): return lax.ppermute(array, axis, pairs)  15 us
    all_to_all x1, starting transfers between devices, branch(): returned = exchange(results)  9.35 us
    pallas_call x1, Pallas kernels, temporal(): pl.pallas_call(kernel, out_shape=jax.ShapeDtypeStruct(rows_in.shape, BF16...  6.71 us
    all_to_all x1, starting transfers between devices, branch(): framed = exchange(*packed)  6.37 us
    pallas_call x1, Pallas kernels, spatial(): pl.pallas_call(kernel, out_shape=[whole, whole, jax.ShapeDtypeStruct((slo...  5.19 us
    pallas_call x1, Pallas kernels, finish(): pl.pallas_call(kernel, out_shape=[jax.ShapeDtypeStruct((count, heads * DH...  4.94 us
  transfers between devices with their start and end apart: 7, of which 2 were waited for; matrix products, arithmetic and copies ran while one was open for 0% of the time, Pallas kernels for 11%

profile of v4, /device:TPU:14, one launch (start us, length us, event | category | flops | bytes accessed | tf_op | source)
XLA Modules:
  0.0 132.7 jit_solution(1581867140502101309)
XLA Ops:
  0.6 1.4 %fusion = s32[]{:T(128)} fusion(s32[24]{0:T(128)} %param.17, s32[]{:T(128)S(6)} %select_n.3), kind=kLoop, calls=%fused_computation.1 | loop fusion | flops 17 | bytes 32 | tf_op jit(solution)/shard_map/reduce_sum | solution.py:432
  2.7 129.9 %conditional.1 = ((bf16[512,768]{1,0:T(8,128)(2,1)}, bf16[512,768]{1,0:T(8,128)(2,1)}, bf16[512,768]{1,0:T(8,128)(2,1)}, bf16[512,768]{1,0:T(8,128)(2,1)})) conditional(s32[]{:T(128)} %clamp.3, (bf16[1,512,768]{2,1,0:T(8,128)(2,1)}, bf16[1,512,768]{2,1,0:T(8,128)(2,1)}, bf16[1,512,768]{2,1,0:T(8,128)(2,1)}, ...), branch_computations={%region_1.0_spmd, %region_2.0_spmd, %region_3.0_spmd, %region_4.0_... | conditional | flops 211342180352 | bytes 56722168 | solution.py:437
  2.9 3.6 %pack_temporal.10.refs_4_ = bf16[8,4,5,64,128]{4,3,2,1,0:T(8,128)(2,1)} custom-call(s32[24]{0:T(128)} %get-tuple-element.323.kind_ref, s32[1]{0:T(128)} %get-tuple-element.324.first_ref, bf16[8,64,768]{2,1,0:T(8,128)(2,1)} %bitcast.146, bf16[8,64,768]{2,1,0:T(8,128)(2,1)} %bitcast.93, bf16[8,64,768]{2,1,0:T(8,128)(2,1)} %bitcast.122, ...), custom_call_target="tpu_custom_call" | custom-call | bytes 5242880 | tf_op jit(solution)/shard_map/cond/branch_5_fun/pack_temporal/pallas_call | solution.py:121
  6.6 0.0 copy-start.12
  6.6 0.0 copy-start.20
  6.6 0.0 copy-start.27
  6.6 6.4 %all-to-all-start.8 = ((bf16[8,4,5,64,128]{4,3,2,1,0:T(8,128)(2,1)}), bf16[8,4,5,64,128]{4,3,2,1,0:T(8,128)(2,1)}, u32[]{:S(2)}, u32[]{:S(2)}) async-start(bf16[8,4,5,64,128]{4,3,2,1,0:T(8,128)(2,1)} %pack_temporal.10.refs_4_), calls=%async_computation.8 | async-start | bytes 5242880 | tf_op jit(solution)/shard_map/cond/branch_5_fun/all_to_all | solution.py:409
  13.0 0.0 copy-done.12
  13.0 0.0 copy-done.20
  13.0 0.0 copy-done.27
  13.0 0.0 copy-start.38
  13.0 2.4 %pack_spatial.11 = (bf16[1,8,64,128]{3,2,1,0:T(8,128)(2,1)}, bf16[1,8,64,128]{3,2,1,0:T(8,128)(2,1)}, bf16[1,8,64,128]{3,2,1,0:T(8,128)(2,1)}, bf16[1,8,64,128]{3,2,1,0:T(8,128)(2,1)}) custom-call(s32[24]{0:T(128)S(1)} %copy-done.27, s32[1]{0:T(128)} %get-tuple-element.324.first_ref, bf16[8,64,768]{2,1,0:T(8,128)(2,1)S(1)} %bitcast.94, ...), custom_call_target="tpu_custom_call" | custom-call | bytes 1048576 | tf_op jit(solution)/shard_map/cond/branch_5_fun/pack_spatial/pallas_call | solution.py:89
  15.4 3.4 %collective-permute-start.25 = (bf16[1,8,64,128]{3,2,1,0:T(8,128)(2,1)}, bf16[1,8,64,128]{3,2,1,0:T(8,128)(2,1)S(1)}, u32[]{:S(2)}, u32[]{:S(2)}) collective-permute-start(bf16[1,8,64,128]{3,2,1,0:T(8,128)(2,1)} %get-tuple-element.335), channel_id=1, source_target_pairs={{0,4},{4,8},{8,12},{12,16},{16,20},{20,24},{24,28},{1,5},{5,9},{9,... | collective-permute-start | bytes 393224 | tf_op jit(solution)/shard_map/cond/branch_5_fun/ppermute | solution.py:390
  18.8 3.4 %collective-permute-start.26 = (bf16[1,8,64,128]{3,2,1,0:T(8,128)(2,1)}, bf16[1,8,64,128]{3,2,1,0:T(8,128)(2,1)}, u32[]{:S(2)}, u32[]{:S(2)}) collective-permute-start(bf16[1,8,64,128]{3,2,1,0:T(8,128)(2,1)} %get-tuple-element.336), channel_id=1, source_target_pairs={{0,4},{4,8},{8,12},{12,16},{16,20},{20,24},{24,28},{1,5},{5,9},{9,... | collective-permute-start | bytes 393224 | tf_op jit(solution)/shard_map/cond/branch_5_fun/ppermute | solution.py:390
  22.2 2.5 %collective-permute-start.27 = (bf16[1,8,64,128]{3,2,1,0:T(8,128)(2,1)}, bf16[1,8,64,128]{3,2,1,0:T(8,128)(2,1)S(1)}, u32[]{:S(2)}, u32[]{:S(2)}) collective-permute-start(bf16[1,8,64,128]{3,2,1,0:T(8,128)(2,1)} %get-tuple-element.337), channel_id=1, source_target_pairs={{4,0},{8,4},{12,8},{16,12},{20,16},{24,20},{28,24},{5,1},{9,5},{13... | collective-permute-start | bytes 393224 | tf_op jit(solution)/shard_map/cond/branch_5_fun/ppermute | solution.py:390
  24.6 3.4 %collective-permute-start.28 = (bf16[1,8,64,128]{3,2,1,0:T(8,128)(2,1)}, bf16[1,8,64,128]{3,2,1,0:T(8,128)(2,1)S(1)}, u32[]{:S(2)}, u32[]{:S(2)}) collective-permute-start(bf16[1,8,64,128]{3,2,1,0:T(8,128)(2,1)} %get-tuple-element.338), channel_id=1, source_target_pairs={{4,0},{8,4},{12,8},{16,12},{20,16},{24,20},{28,24},{5,1},{9,5},{13... | collective-permute-start | bytes 393224 | tf_op jit(solution)/shard_map/cond/branch_5_fun/ppermute | solution.py:390
  28.0 38.2 %all-to-all-done.8.rows_ref = bf16[8,4,5,64,128]{4,3,2,1,0:T(8,128)(2,1)} async-done(((bf16[8,4,5,64,128]{4,3,2,1,0:T(8,128)(2,1)}), bf16[8,4,5,64,128]{4,3,2,1,0:T(8,128)(2,1)}, u32[]{:S(2)}, u32[]{:S(2)}) %all-to-all-start.8) | async-done | bytes 2621472 | tf_op jit(solution)/shard_map/cond/branch_5_fun/all_to_all | solution.py:409
  66.2 0.0 copy-done.38
  66.2 6.7 %temporal.10 = bf16[8,4,5,64,128]{4,3,2,1,0:T(8,128)(2,1)} custom-call(s32[24]{0:T(128)S(1)} %copy-done.27, s32[1]{0:T(128)} %get-tuple-element.324.first_ref, s32[24]{0:T(128)S(1)} %copy-done.38, bf16[8,4,5,64,128]{4,3,2,1,0:T(8,128)(2,1)} %all-to-all-done.8.rows_ref), custom_call_target="tpu_custom_call" | custom-call | flops 10000000000 | bytes 5242880 | tf_op jit(solution)/shard_map/cond/branch_5_fun/temporal/pallas_call | solution.py:200
  72.9 0.0 copy-start.21
  72.9 9.3 %all-to-all-start.9 = ((bf16[8,4,5,64,128]{4,3,2,1,0:T(8,128)(2,1)}), bf16[8,4,5,64,128]{4,3,2,1,0:T(8,128)(2,1)}, u32[]{:S(2)}, u32[]{:S(2)}) async-start(bf16[8,4,5,64,128]{4,3,2,1,0:T(8,128)(2,1)} %temporal.10), calls=%async_computation.9 | async-start | bytes 5242880 | tf_op jit(solution)/shard_map/cond/branch_5_fun/all_to_all | solution.py:411
  82.3 0.0 collective-permute-done.25
  82.3 0.0 copy-start.33
  82.3 0.0 collective-permute-done.26
  82.3 0.0 collective-permute-done.27
  82.3 0.0 collective-permute-done.28
  82.3 0.6 copy-done.33
  83.0 0.0 copy-done.21
  83.0 5.2 %spatial.11 = (bf16[512,768]{1,0:T(8,128)(2,1)}, bf16[512,768]{1,0:T(8,128)(2,1)}, f32[1,2,512,128]{3,2,1,0:T(8,128)}, f32[1,2,512]{2,1,0:T(2,128)}) custom-call(s32[24]{0:T(128)S(1)} %copy-done.27, s32[1]{0:T(128)} %get-tuple-element.324.first_ref, s32[1]{0:T(128)} %get-tuple-element.330.frame_ref, bf16[512,768]{1,0:T(8,128)(2,1)S(1)} %bitcast.148, ...), custom_call_target="tpu_custom_call" | custom-call | flops 199999995904 | bytes 1048576 | tf_op jit(solution)/shard_map/cond/branch_5_fun/spatial/pallas_call | solution.py:262
  88.1 2.5 %collective-permute-start.29 = (f32[1,2,512]{2,1,0:T(2,128)}, f32[1,2,512]{2,1,0:T(2,128)S(1)}, u32[]{:S(2)}, u32[]{:S(2)}) collective-permute-start(f32[1,2,512]{2,1,0:T(2,128)} %get-tuple-element.345), channel_id=1, source_target_pairs={{4,0},{8,4},{12,8},{16,12},{20,16},{24,20},{28,24},{5,1},{9,5},{13... | collective-permute-start | bytes 12296 | tf_op jit(solution)/shard_map/cond/branch_5_fun/ppermute | solution.py:390
  90.6 35.9 %collective-permute-done.29.refs_7_ = f32[1,2,512]{2,1,0:T(2,128)S(1)} collective-permute-done((f32[1,2,512]{2,1,0:T(2,128)}, f32[1,2,512]{2,1,0:T(2,128)S(1)}, u32[]{:S(2)}, u32[]{:S(2)}) %collective-permute-start.29) | collective-permute-done | bytes 4128 | tf_op jit(solution)/shard_map/cond/branch_5_fun/ppermute | solution.py:390
  126.6 0.0 all-to-all-done.9.refs_0_
  126.6 0.0 copy-start.5
  126.6 1.0 copy-done.5
  127.6 4.9 %finish.12 = (bf16[512,768]{1,0:T(8,128)(2,1)}, bf16[512,768]{1,0:T(8,128)(2,1)}, bf16[512,768]{1,0:T(8,128)(2,1)}, bf16[512,768]{1,0:T(8,128)(2,1)}) custom-call(s32[24]{0:T(128)S(1)} %copy-done.27, s32[1]{0:T(128)} %get-tuple-element.324.first_ref, ...), custom_call_target="tpu_custom_call", output_to_operand_aliasing={{0}: (3, {}), {1}: (4, {})} | custom-call | flops 268435456 | bytes 6291456 | tf_op jit(solution)/shard_map/cond/branch_5_fun/finish/pallas_call | solution.py:373
Async XLA Ops:
  6.6 6.4 %copy-start.12 = (bf16[1,512,768]{2,1,0:T(8,128)(2,1)S(1)}, bf16[1,512,768]{2,1,0:T(8,128)(2,1)}, u32[]{:S(2)}) copy-start(bf16[1,512,768]{2,1,0:T(8,128)(2,1)} %get-tuple-element.332) | copy-start | bytes 2359300 | tf_op jit(solution)/shard_map/cond
  6.6 6.4 %copy-start.20 = (bf16[1,512,768]{2,1,0:T(8,128)(2,1)S(1)}, bf16[1,512,768]{2,1,0:T(8,128)(2,1)}, u32[]{:S(2)}) copy-start(bf16[1,512,768]{2,1,0:T(8,128)(2,1)} %get-tuple-element.333) | copy-start | bytes 2359300 | tf_op jit(solution)/shard_map/cond
  6.6 6.4 %copy-start.27 = (s32[24]{0:T(128)S(1)}, s32[24]{0:T(128)}, u32[]{:S(2)}) copy-start(s32[24]{0:T(128)} %get-tuple-element.323.kind_ref) | copy-start | bytes 292 | tf_op jit(solution)/shard_map/cond
  6.6 59.6 %all-to-all-start.8 = ((bf16[8,4,5,64,128]{4,3,2,1,0:T(8,128)(2,1)}), bf16[8,4,5,64,128]{4,3,2,1,0:T(8,128)(2,1)}, u32[]{:S(2)}, u32[]{:S(2)}) async-start(bf16[8,4,5,64,128]{4,3,2,1,0:T(8,128)(2,1)} %pack_temporal.10.refs_4_), calls=%async_computation.8 | async-start | bytes 5242880 | tf_op jit(solution)/shard_map/cond/branch_5_fun/all_to_all | solution.py:409
  13.0 53.2 %copy-start.38 = (s32[24]{0:T(128)S(1)}, s32[24]{0:T(128)}, u32[]{:S(2)}) copy-start(s32[24]{0:T(128)} %get-tuple-element.325.band_ref) | copy-start | bytes 292 | tf_op jit(solution)/shard_map/cond
  15.4 66.9 %collective-permute-start.25 = (bf16[1,8,64,128]{3,2,1,0:T(8,128)(2,1)}, bf16[1,8,64,128]{3,2,1,0:T(8,128)(2,1)S(1)}, u32[]{:S(2)}, u32[]{:S(2)}) collective-permute-start(bf16[1,8,64,128]{3,2,1,0:T(8,128)(2,1)} %get-tuple-element.335), channel_id=1, source_target_pairs={{0,4},{4,8},{8,12},{12,16},{16,20},{20,24},{24,28},{1,5},{5,9},{9,... | collective-permute-start | bytes 393224 | tf_op jit(solution)/shard_map/cond/branch_5_fun/ppermute | solution.py:390
  18.8 63.5 %collective-permute-start.26 = (bf16[1,8,64,128]{3,2,1,0:T(8,128)(2,1)}, bf16[1,8,64,128]{3,2,1,0:T(8,128)(2,1)}, u32[]{:S(2)}, u32[]{:S(2)}) collective-permute-start(bf16[1,8,64,128]{3,2,1,0:T(8,128)(2,1)} %get-tuple-element.336), channel_id=1, source_target_pairs={{0,4},{4,8},{8,12},{12,16},{16,20},{20,24},{24,28},{1,5},{5,9},{9,... | collective-permute-start | bytes 393224 | tf_op jit(solution)/shard_map/cond/branch_5_fun/ppermute | solution.py:390
  22.2 60.2 %collective-permute-start.27 = (bf16[1,8,64,128]{3,2,1,0:T(8,128)(2,1)}, bf16[1,8,64,128]{3,2,1,0:T(8,128)(2,1)S(1)}, u32[]{:S(2)}, u32[]{:S(2)}) collective-permute-start(bf16[1,8,64,128]{3,2,1,0:T(8,128)(2,1)} %get-tuple-element.337), channel_id=1, source_target_pairs={{4,0},{8,4},{12,8},{16,12},{20,16},{24,20},{28,24},{5,1},{9,5},{13... | collective-permute-start | bytes 393224 | tf_op jit(solution)/shard_map/cond/branch_5_fun/ppermute | solution.py:390
  24.6 57.7 %collective-permute-start.28 = (bf16[1,8,64,128]{3,2,1,0:T(8,128)(2,1)}, bf16[1,8,64,128]{3,2,1,0:T(8,128)(2,1)S(1)}, u32[]{:S(2)}, u32[]{:S(2)}) collective-permute-start(bf16[1,8,64,128]{3,2,1,0:T(8,128)(2,1)} %get-tuple-element.338), channel_id=1, source_target_pairs={{4,0},{8,4},{12,8},{16,12},{20,16},{24,20},{28,24},{5,1},{9,5},{13... | collective-permute-start | bytes 393224 | tf_op jit(solution)/shard_map/cond/branch_5_fun/ppermute | solution.py:390
  72.9 10.0 %copy-start.21 = (bf16[1,512,768]{2,1,0:T(8,128)(2,1)S(1)}, bf16[1,512,768]{2,1,0:T(8,128)(2,1)}, u32[]{:S(2)}) copy-start(bf16[1,512,768]{2,1,0:T(8,128)(2,1)} %get-tuple-element.331) | copy-start | bytes 2359300 | tf_op jit(solution)/shard_map/cond
  72.9 53.6 %all-to-all-start.9 = ((bf16[8,4,5,64,128]{4,3,2,1,0:T(8,128)(2,1)}), bf16[8,4,5,64,128]{4,3,2,1,0:T(8,128)(2,1)}, u32[]{:S(2)}, u32[]{:S(2)}) async-start(bf16[8,4,5,64,128]{4,3,2,1,0:T(8,128)(2,1)} %temporal.10), calls=%async_computation.9 | async-start | bytes 5242880 | tf_op jit(solution)/shard_map/cond/branch_5_fun/all_to_all | solution.py:411
  82.3 0.7 copy-start.33
  88.1 38.4 %collective-permute-start.29 = (f32[1,2,512]{2,1,0:T(2,128)}, f32[1,2,512]{2,1,0:T(2,128)S(1)}, u32[]{:S(2)}, u32[]{:S(2)}) collective-permute-start(f32[1,2,512]{2,1,0:T(2,128)} %get-tuple-element.345), channel_id=1, source_target_pairs={{4,0},{8,4},{12,8},{16,12},{20,16},{24,20},{28,24},{5,1},{9,5},{13... | collective-permute-start | bytes 12296 | tf_op jit(solution)/shard_map/cond/branch_5_fun/ppermute | solution.py:390
  126.6 1.0 copy-start.5
